TPU v7x, 32 devices: a whole 2x2x4 slice. The times are simulated.
32 devices in a mesh: ctx: 8 (over z, x), head: 4 (over y, core).
Axes of the slice: x: 2, y: 2, z: 4, core: 2. Of those that a mesh axis runs over, the one named last changes fastest.
Arguments:
- query_tokens: bfloat16 [2, 2048, 4, 512], P(None, 'ctx', 'head'), may hold values from -6 to 6
- key_tokens: bfloat16 [2048, 4, 512], P('ctx', 'head'), may hold values from -6 to 6
- value_tokens: bfloat16 [2048, 4, 512], P('ctx', 'head'), may hold values from -6 to 6
- log_rate: float32 [4, 2048], P('head', 'ctx'), may hold values from -1.5 to 0.5
- fast_weights: float32 [4, 3, 512, 512], P('head'), may hold values from -0.25 to 0.25
- norm_gain: float32 [4, 512], P('head'), may hold values from 0.5 to 1.5
- out_grad: bfloat16 [2, 2048, 4, 512], P(None, 'ctx', 'head'), may hold values from -0.75 to 0.75
Outputs:
- grad_query: bfloat16 [2, 2048, 4, 512], P(None, 'ctx', 'head')
- grad_key: bfloat16 [2048, 4, 512], P('ctx', 'head')
- grad_value: bfloat16 [2048, 4, 512], P('ctx', 'head')
- grad_rate: float32 [4, 2048], P('head', 'ctx')
- grad_weights: float32 [4, 3, 512, 512], P('head', None, 'ctx')
- grad_gain: float32 [4, 512], P('head', 'ctx')
All inputs are finite; a program needn't handle non-finite values.
Results may differ from a plain program's by a relative error of at most 0.0012.
Values sent between devices are 32-bit elements; how exact they have to be, the bound alone decides.
No kernel may reach another device: no remote copies, remote signals or barrier semaphores. Data moves between devices by JAX's collectives and lax.ppermute only.
A program may use at most 128 MiB of HBM per device.

v0:
```python
from functools import partial

import jax
import jax.numpy as jnp
from jax import lax
from jax.sharding import PartitionSpec as P

EPSILON = 1e-06
PRECISE = lax.Precision.HIGHEST


def apply_fast(weights, inputs):
    gate_pre = jnp.dot(inputs, weights[0].T, precision=PRECISE, preferred_element_type=jnp.float32)
    up_pre = jnp.dot(inputs, weights[1].T, precision=PRECISE, preferred_element_type=jnp.float32)
    hidden = jax.nn.silu(gate_pre) * up_pre
    return jnp.dot(hidden, weights[2], precision=PRECISE, preferred_element_type=jnp.float32)


def update_grad(weights, key_rows, value_rows, rate_log, factor):

    def update_loss(inner):
        rate = jnp.exp(rate_log) * factor
        return -jnp.sum(rate[:, None] * apply_fast(inner, key_rows) * value_rows)

    return jax.grad(update_loss)(weights)


def renorm(update, anchor):
    target = jnp.sqrt(jnp.sum(anchor * anchor, axis=-1) + EPSILON)
    actual = jnp.sqrt(jnp.sum(update * update, axis=-1) + EPSILON)
    return update * (target / actual)[..., None]


def norm_back(outputs, cotan, square_total, product_total, norm_width, gain_row):
    inverse = 1.0 / jnp.sqrt(square_total / norm_width + EPSILON)
    grad_out = (
        gain_row * cotan * inverse[:, None]
        - outputs * (inverse * inverse * inverse * product_total / norm_width)[:, None]
    )
    gain_term = jnp.sum(cotan * outputs * inverse[:, None], axis=0)
    return (grad_out, gain_term)


def local(query_tokens, key_tokens, value_tokens, log_rate, fast_weights, norm_gain, out_grad):
    start_weights = fast_weights[0]
    query_one = query_tokens[0, :, 0, :].astype(jnp.float32)
    query_two = query_tokens[1, :, 0, :].astype(jnp.float32)
    key_rows = key_tokens[:, 0, :].astype(jnp.float32)
    value_rows = value_tokens[:, 0, :].astype(jnp.float32)
    cotan_one = out_grad[0, :, 0, :].astype(jnp.float32)
    cotan_two = out_grad[1, :, 0, :].astype(jnp.float32)
    gain_row = norm_gain[0]
    shards = lax.axis_size("ctx")
    tokens_here = key_rows.shape[0]
    head_dim = key_rows.shape[1]
    factor = (tokens_here * shards * head_dim) ** (-0.5)
    row_count = start_weights.shape[1] // shards
    offset = lax.axis_index("ctx") * row_count
    norm_width = lax.axis_size("head") * head_dim
    local_grad, update_back = jax.vjp(
        partial(update_grad, factor=factor), start_weights, key_rows, value_rows, log_rate[0]
    )
    total_grad = lax.psum(local_grad, "ctx")
    new_weights, renorm_back = jax.vjp(renorm, start_weights - total_grad, start_weights)
    out_one, apply_back_one = jax.vjp(apply_fast, start_weights, query_one)
    out_two, apply_back_two = jax.vjp(apply_fast, new_weights, query_two)
    square_one = jnp.sum(out_one * out_one, axis=1)
    product_one = jnp.sum(gain_row * cotan_one * out_one, axis=1)
    square_two = jnp.sum(out_two * out_two, axis=1)
    product_two = jnp.sum(gain_row * cotan_two * out_two, axis=1)
    squares, products = lax.psum(
        (jnp.stack([square_one, square_two]), jnp.stack([product_one, product_two])), "head"
    )
    square_one, square_two = (squares[0], squares[1])
    product_one, product_two = (products[0], products[1])
    grad_out_one, gain_one = norm_back(
        out_one, cotan_one, square_one, product_one, norm_width, gain_row
    )
    grad_out_two, gain_two = norm_back(
        out_two, cotan_two, square_two, product_two, norm_width, gain_row
    )
    weight_two, query_grad_two = apply_back_two(grad_out_two)
    weight_one, query_grad_one = apply_back_one(grad_out_one)
    cot_total = lax.psum(weight_two, "ctx")
    update_cot, anchor_cot = renorm_back(cot_total)
    direct_rows = lax.dynamic_slice_in_dim(update_cot + anchor_cot, offset, row_count, 1)
    weight_part, key_grad, value_grad, rate_grad = update_back(-update_cot)
    summed, gain_sum = (
        lax.psum_scatter(weight_one + weight_part, "ctx", scatter_dimension=1, tiled=True),
        lax.psum_scatter((gain_one + gain_two)[None, :], "ctx", scatter_dimension=1, tiled=True),
    )
    grad_query = jnp.stack([query_grad_one, query_grad_two])[:, :, None, :].astype(jnp.bfloat16)
    grad_key = key_grad[:, None, :].astype(jnp.bfloat16)
    grad_value = value_grad[:, None, :].astype(jnp.bfloat16)
    grad_rate = rate_grad[None, :]
    grad_weights = (summed + direct_rows)[None]
    return (grad_query, grad_key, grad_value, grad_rate, grad_weights, gain_sum)


def solution(mesh):
    placed = (
        P(None, "ctx", "head", None),
        P("ctx", "head", None),
        P("ctx", "head", None),
        P("head", "ctx"),
        P("head", None, None, None),
        P("head", None),
        P(None, "ctx", "head", None),
    )
    return jax.shard_map(
        local,
        mesh=mesh,
        in_specs=placed,
        out_specs=(
            P(None, "ctx", "head", None),
            P("ctx", "head", None),
            P("ctx", "head", None),
            P("head", "ctx"),
            P("head", None, "ctx", None),
            P("head", "ctx"),
        ),
        check_vma=False,
    )
```

profile of v0, /device:TPU:0, one launch (start us, length us, event | category | flops | bytes accessed | tf_op | source)
XLA Modules:
  0.0 459.2 jit_solution(13694797393387965135)
XLA Ops:
  7.2 0.8 broadcast_multiply_fusion.2
  8.1 2.0 fusion.17
  10.1 2.6 fusion.10
  14.2 1.2 convolution_bitcast_fusion.11
  16.2 2.0 pad_add_fusion.1
  18.3 1.6 fusion.19
  19.9 1.8 fusion.25
  21.8 0.8 copy-done.42
  22.6 2.0 multiply_reduce_fusion.4
  24.6 125.4 %all-reduce.15.cloned.1.call-done = f32[3,512,512]{2,1,0:T(8,128)} async-done(((f32[3,512,512]{2,1,0:T(8,128)}), f32[3,512,512]{2,1,0:T(8,128)}) %all-reduce.15.cloned.1.call-update) | async-done | bytes 3145744 | tf_op jit(solution)/shard_map/psum | solution.py:63
  149.9 2.5 multiply_reduce_fusion.1
  152.8 1.4 copy-done.2
  155.6 2.0 multiply_reduce_fusion.3
  157.6 7.1 %psum.29 = f32[2,256]{1,0:T(2,128)S(1)} all-reduce(f32[2,256]{1,0:T(2,128)S(1)} %pad_maximum_fusion.1), channel_id=1, replica_groups=mesh['ctx'=8,'head'=4] {'head'}, use_global_device_ids=true, to_apply=%region_5.6 | all-reduce | flops 512 | bytes 4096 | tf_op jit(solution)/shard_map/psum | solution.py:71
  164.7 1.8 fusion.62
  166.5 5.9 %psum.30 = f32[2,256]{1,0:T(2,128)S(1)} all-reduce(f32[2,256]{1,0:T(2,128)S(1)} %pad_maximum_fusion.2), channel_id=1, replica_groups=mesh['ctx'=8,'head'=4] {'head'}, use_global_device_ids=true, to_apply=%region_8.9 | all-reduce | flops 512 | bytes 4096 | tf_op jit(solution)/shard_map/psum | solution.py:71
  172.4 2.7 fusion.28
  175.2 2.2 convolution_bitcast_fusion.6
  178.2 1.3 convolution_bitcast_fusion.8
  179.5 2.0 pad_add_fusion
  181.5 0.9 copy.25
  182.4 2.4 fusion.8
  184.8 3.0 convolution_bitcast_fusion.4
  187.9 2.3 convolution_bitcast_fusion.5
  190.2 1.8 convolution_bitcast_fusion.3
  192.0 116.4 %all-reduce.17.cloned.1.call-done = f32[3,512,512]{2,1,0:T(8,128)} async-done(((f32[3,512,512]{2,1,0:T(8,128)}), f32[3,512,512]{2,1,0:T(8,128)}) %all-reduce.17.cloned.1.call-update) | async-done | bytes 3145744 | tf_op jit(solution)/shard_map/psum | solution.py:84
  308.5 3.3 multiply_reduce_fusion
  312.2 1.0 copy-done.7
  313.2 2.2 fusion.167
  316.2 1.1 fusion.31
  318.2 1.3 multiply_add_fusion
  320.9 1.2 convolution_bitcast_fusion.2
  322.1 2.4 add_add_fusion.1
  324.5 2.8 fusion.27
  327.3 3.0 fusion.4
  330.4 1.2 fusion.15
  331.6 1.3 fusion.5
  332.8 0.8 pad_maximum_fusion
  333.7 38.9 %reduce-scatter.7.cloned.1.call-done = f32[64,1]{1,0:T(8,128)} async-done(((f32[512,1]{1,0:T(8,128)}), f32[64,1]{1,0:T(8,128)}) %reduce-scatter.7.cloned.1.call-update) | async-done | bytes 272
  372.6 1.3 copy.26
  374.0 3.1 fusion.30
  377.1 2.7 convolution_add_fusion.3
  379.9 1.1 convolution_add_fusion.2
  380.9 1.8 fusion.3
  382.7 1.0 fusion.6
  383.8 2.0 fusion.57
  386.4 63.9 %reduce-scatter.5.cloned.1.call-done = f32[3,64,512]{2,1,0:T(8,128)} async-done(((f32[3,512,512]{2,1,0:T(8,128)}), f32[3,64,512]{2,1,0:T(8,128)}) %reduce-scatter.5.cloned.1.call-update) | async-done | bytes 393232 | tf_op jit(solution)/shard_map/reduce_scatter | solution.py:89
  450.3 2.0 fusion.78
  (135 shorter events, 9.0 us)
Async XLA Ops:
  7.2 5.5 %copy-start.1 = (f32[1,3,512,512]{3,2,1,0:T(8,128)S(1)}, f32[1,3,512,512]{3,2,1,0:T(8,128)}, u32[]{:S(2)}) copy-start(f32[1,3,512,512]{3,2,1,0:T(8,128)} %param.11) | copy-start | bytes 9437188
  7.2 142.7 %all-reduce.15.cloned.1.call-start = ((), (), s32[]{:S(2)}) async-start(), calls=%async_computation.2 | async-start | bytes 6291456 | tf_op jit(solution)/shard_map/psum | solution.py:63
  10.1 4.0 copy-start.16
  13.4 2.0 copy-start.23
  13.4 2.0 copy-start.35
  13.5 2.0 copy-start.37
  18.2 290.2 %all-reduce.17.cloned.1.call-start = ((), (), s32[]{:S(2)}) async-start(), calls=%async_computation.3 | async-start | bytes 6291456 | tf_op jit(solution)/shard_map/psum | solution.py:84
  154.1 3.5 copy-start.4
  154.1 10.5 %copy-start.52 = (f32[1,512]{1,0:T(1,128)S(1)}, f32[1,512]{1,0:T(1,128)}, u32[]{:S(2)}) copy-start(f32[1,512]{1,0:T(1,128)} %param.12) | copy-start | bytes 6148
  154.9 2.7 copy-start.45
  155.6 2.0 copy-start.47
  172.4 5.0 %copy-start.14 = (bf16[2,256,1,512]{3,1,2,0:T(8,128)(2,1)S(1)}, bf16[2,256,1,512]{3,1,2,0:T(8,128)(2,1)}, u32[]{:S(2)}) copy-start(bf16[2,256,1,512]{3,1,2,0:T(8,128)(2,1)} %param.7) | copy-start | bytes 1572868
  172.4 5.0 %copy-start.48 = (f32[256,512]{1,0:T(8,128)S(1)}, f32[256,512]{1,0:T(8,128)}, u32[]{:S(2)}) copy-start(f32[256,512]{1,0:T(8,128)} %copy-done.47) | copy-start | bytes 1572868
  175.1 3.0 copy-start.49
  175.1 3.0 copy-start.21
  175.1 3.0 copy-start.31
  175.2 3.0 copy-start.46
  181.5 191.1 %reduce-scatter.7.cloned.1.call-start = ((), (), s32[]{:S(2)}) async-start(), calls=%async_computation.5 | async-start | bytes 294912
  182.4 5.5 %copy-start.22 = (bf16[2,256,1,512]{3,1,2,0:T(8,128)(2,1)S(1)}, bf16[2,256,1,512]{3,1,2,0:T(8,128)(2,1)}, u32[]{:S(2)}) copy-start(bf16[2,256,1,512]{3,1,2,0:T(8,128)(2,1)} %param.13) | copy-start | bytes 1572868
  182.4 5.5 %copy-start.30 = (f32[256,512]{1,0:T(8,128)S(1)}, f32[256,512]{1,0:T(8,128)}, u32[]{:S(2)}) copy-start(f32[256,512]{1,0:T(8,128)} %get-tuple-element.36) | copy-start | bytes 1572868
  182.4 5.5 %copy-start.40 = (f32[256,512]{1,0:T(8,128)S(1)}, f32[256,512]{1,0:T(8,128)}, u32[]{:S(2)}) copy-start(f32[256,512]{1,0:T(8,128)} %copy-done.39) | copy-start | bytes 1572868
  182.4 5.5 %copy-start.43 = (f32[256,512]{1,0:T(8,128)S(1)}, f32[256,512]{1,0:T(8,128)}, u32[]{:S(2)}) copy-start(f32[256,512]{1,0:T(8,128)} %copy-done.42) | copy-start | bytes 1572868
  184.8 7.1 %copy-start.50 = (f32[256,512]{1,0:T(8,128)}, f32[256,512]{1,0:T(8,128)S(1)}, u32[]{:S(2)}) copy-start(f32[256,512]{1,0:T(8,128)S(1)} %fusion.8) | copy-start | bytes 1572868
  184.8 5.3 %copy-start.15 = (bf16[2,256,1,512]{3,1,2,0:T(8,128)(2,1)S(1)}, bf16[2,256,1,512]{3,1,2,0:T(8,128)(2,1)}, u32[]{:S(2)}) copy-start(bf16[2,256,1,512]{3,1,2,0:T(8,128)(2,1)} %param.7) | copy-start | bytes 1572868
  192.0 258.3 %reduce-scatter.5.cloned.1.call-start = ((), (), s32[]{:S(2)}) async-start(), calls=%async_computation.4 | async-start | bytes 3538944 | tf_op jit(solution)/shard_map/reduce_scatter | solution.py:89
  308.5 3.7 copy-start.3
  308.5 4.7 %copy-start.7 = (f32[3,512,512]{2,1,0:T(8,128)S(1)}, f32[3,512,512]{2,1,0:T(8,128)}, u32[]{:S(2)}) copy-start(f32[3,512,512]{2,1,0:T(8,128)} %all-reduce.17.cloned.1.call-done) | copy-start | bytes 9437188
  313.2 3.0 copy-start.11
  315.4 4.1 copy-start.5
  315.4 1.9 copy-start.9
  315.4 1.9 copy-start.17
  315.4 2.5 copy-start.24
  315.4 2.6 copy-start.36
  315.4 2.8 copy-start.38
  319.5 2.5 copy-start.32
  319.5 2.5 copy-start.33
  319.5 2.5 copy-start.34
  324.5 5.9 %copy-start.44 = (f32[256,512]{1,0:T(8,128)S(1)}, f32[256,512]{1,0:T(8,128)}, u32[]{:S(2)}) copy-start(f32[256,512]{1,0:T(8,128)} %copy-done.42) | copy-start | bytes 1572868
  324.5 5.9 %copy-start.51 = (f32[256,512]{1,0:T(8,128)S(1)}, f32[256,512]{1,0:T(8,128)}, u32[]{:S(2)}) copy-start(f32[256,512]{1,0:T(8,128)} %copy-done.50) | copy-start | bytes 1572868
  327.3 4.2 copy-start.41
  373.9 3.1 copy-start.6
  374.0 5.8 %copy-start.20 = (f32[256,512]{1,0:T(8,128)S(1)}, f32[256,512]{1,0:T(8,128)}, u32[]{:S(2)}) copy-start(f32[256,512]{1,0:T(8,128)} %copy-done.19) | copy-start | bytes 1572868
  377.1 3.8 copy-start.29
  379.8 2.9 copy-start.27
  379.8 3.9 copy-start.12
  379.8 3.9 copy-start.18
  379.8 3.9 copy-start.25
  382.7 3.1 copy-start.53
  (10 other events, 13.9 us)
Sparse Core Ops, SparseCore 0:
  18.4 131.5 all-reduce.14
  181.6 126.8 all-reduce.16
  312.4 60.1 reduce-scatter.6
  376.1 74.1 reduce-scatter.4
where the time goes:
time: 468 us; the launch traced here: 459 us
  waiting for transfers between devices  345 us (74%)
  matrix products  58.4 us (12%)
  other arithmetic  20.9 us (4%)
  between operations  15.1 us (3%)
  blocking collectives  12.9 us (3%)
  local copies, waits for them, and re-layouts  6.94 us (1%)
    psum x1, waiting for transfers between devices, local(): total_grad = lax.psum(local_grad, 'ctx')  125 us
    psum x1, waiting for transfers between devices, local(): cot_total = lax.psum(weight_two, 'ctx')  116 us
    reduce_scatter x1, waiting for transfers between devices, local(): lax.psum_scatter(weight_one + weight_part, 'ctx', scatter_dimension=1, ti...  63.9 us
    unnamed x5, waiting for transfers between devices  39 us
    dot_general x12, matrix products, apply_fast(): jnp.dot(hidden, weights[2], precision=PRECISE, preferred_element_type=jnp...  21.7 us
    dot_general x12, matrix products, apply_fast(): jnp.dot(inputs, weights[0].T, precision=PRECISE, preferred_element_type=j...  18.4 us
    dot_general x12, matrix products, apply_fast(): jnp.dot(inputs, weights[1].T, precision=PRECISE, preferred_element_type=j...  18.3 us
    psum x2, blocking collectives, local(): lax.psum((jnp.stack([square_one, square_two]), jnp.stack([product_one, pr...  12.9 us
  transfers between devices with their start and end apart: 4, of which 4 were waited for; matrix products, arithmetic and copies ran while one was open for 11% of the time, Pallas kernels for 0%

commit v1 on v0

v1 whole, which is shorter than its diff:
```python
from functools import partial

import jax
import jax.numpy as jnp
import numpy as np
from jax import lax
from jax.experimental import pallas as pl
from jax.experimental.pallas import tpu as pltpu
from jax.sharding import PartitionSpec as P

EPSILON = 1e-06
SETS = 2
VMEM_BYTES = 48 * 1024 * 1024
f32, bf16 = jnp.float32, jnp.bfloat16


def ring_order(count):
    width = max(w for w in range(1, count + 1) if count % w == 0 and w * w <= count)
    height = count // width
    if width == 1 or height % 2:
        return list(range(count))
    order = [0]
    for row in range(height):
        columns = range(1, width) if row % 2 == 0 else range(width - 1, 0, -1)
        order += [row * width + column for column in columns]
    return order + [row * width for row in range(height - 1, 0, -1)]


def ring_tables(count, heads):
    order = ring_order(count)
    pairs = []
    for head in range(heads):
        way = order if head % 2 == 0 else order[::-1]
        for at in range(count):
            pairs.append((way[at] * heads + head, way[(at + 1) % count] * heads + head))
    owner = np.zeros((2, count, count), np.int32)
    for parity in range(2):
        way = order if parity == 0 else order[::-1]
        for at in range(count):
            for step in range(count):
                owner[parity, way[at], step] = way[(at - 1 - step) % count]
    return pairs, owner


def pair(x):
    high = x.astype(bf16)
    return high, (x - high.astype(f32)).astype(bf16)


def nt(a, b):
    return lax.dot_general(a, b, (((1,), (1,)), ((), ())), preferred_element_type=f32)


def nn(a, b):
    return lax.dot_general(a, b, (((1,), (0,)), ((), ())), preferred_element_type=f32)


def tn(a, b):
    return lax.dot_general(a, b, (((0,), (0,)), ((), ())), preferred_element_type=f32)


def three(dot, a, b):
    (a_high, a_low), (b_high, b_low) = a, b
    return dot(a_high, b_high) + (dot(a_high, b_low) + dot(a_low, b_high))


def rows_by(x, mats):
    pairs = [pair(m) for m in mats]
    stacked = jnp.concatenate([p[0] for p in pairs] + [p[1] for p in pairs], axis=0)
    both = nt(x, stacked)
    half = both.shape[1] // 2
    total = both[:, :half] + both[:, half:]
    rows = mats[0].shape[0]
    return [total[:, i * rows : (i + 1) * rows] for i in range(len(mats))]


def sums_by(parts, x):
    pairs = [pair(m) for m in parts]
    stacked = jnp.concatenate([p[0] for p in pairs] + [p[1] for p in pairs], axis=1)
    both = tn(stacked, x)
    half = both.shape[0] // 2
    total = both[:half] + both[half:]
    rows = parts[0].shape[1]
    return [total[i * rows : (i + 1) * rows] for i in range(len(parts))]


def silu_parts(gate):
    sig = 1.0 / (1.0 + jnp.exp(-gate))
    act = gate * sig
    return sig, act, sig + act * (1.0 - sig)


def to_columns(rows):
    count, tokens = rows.shape
    if count < 128:
        rows = jnp.concatenate([rows, jnp.zeros((128 - count, tokens), f32)], axis=0)
    turned = jnp.transpose(rows)
    return [turned[:, i : i + 1] for i in range(count)]


def to_rows(columns):
    tokens = columns[0].shape[0]
    lane = lax.broadcasted_iota(jnp.int32, (tokens, 128), 1)
    packed = jnp.zeros((tokens, 128), f32)
    for i, column in enumerate(columns):
        packed = jnp.where(lane == i, column, packed)
    return jnp.transpose(packed)[:8]


def minus_rate(rate_ref, factor):
    return -jnp.exp(to_columns(rate_ref[...])[0]) * factor


def update_kernel(factor, chunks, sets, owner_ref, weights_ref, key_ref, value_ref, rate_ref, placed_ref, *parts_ref):
    rows = weights_ref.shape[1] // chunks
    piece = rows // sets
    for step in range(chunks):
        placed_ref[:, step * rows : (step + 1) * rows, :] = weights_ref[:, pl.ds(pl.multiple_of(owner_ref[step] * rows, rows), rows), :]
    keys, values = key_ref[...], value_ref[...]
    gate, up = rows_by(keys, [placed_ref[0], placed_ref[1]])
    (back,) = rows_by(values, [placed_ref[2]])
    rate = minus_rate(rate_ref, factor)
    _, act, slope = silu_parts(gate)
    back = back * rate
    grad_gate, grad_up = sums_by([back * up * slope, back * act], keys)
    (grad_down,) = sums_by([act * up * rate], values)
    for step in range(chunks):
        for part in range(sets):
            at = step * rows + part * piece
            out = parts_ref[step * sets + part]
            out[0] = grad_gate[at : at + piece]
            out[1] = grad_up[at : at + piece]
            out[2] = grad_down[at : at + piece]


def scales(update, anchor):
    target = jnp.sqrt(jnp.sum(anchor * anchor, axis=-1, keepdims=True) + EPSILON)
    actual = jnp.sqrt(jnp.sum(update * update, axis=-1, keepdims=True) + EPSILON)
    return target, actual


def renorm_kernel(arrived_ref, mine_ref, anchor_ref, update_ref, new_ref):
    anchor = anchor_ref[...]
    update = anchor - (arrived_ref[...] + mine_ref[...])
    target, actual = scales(update, anchor)
    update_ref[...] = update
    new_ref[...] = update * (target / actual)


def renorm_back_kernel(sets, anchor_ref, *refs):
    arrived, mine, updates = refs[:sets], refs[sets : 2 * sets], refs[2 * sets : 3 * sets]
    turned_ref, direct_ref = refs[3 * sets :]
    piece = updates[0].shape[1]
    for part in range(sets):
        at = pl.ds(part * piece, piece)
        anchor = anchor_ref[:, at, :]
        update = updates[part][...]
        cot = arrived[part][...] + mine[part][...]
        target, actual = scales(update, anchor)
        inner = jnp.sum(update * cot, axis=-1, keepdims=True)
        ratio = target / actual
        update_cot = ratio * cot - update * (inner * ratio / (actual * actual))
        turned_ref[:, at, :] = -update_cot
        direct_ref[:, at, :] = update_cot + anchor * (inner / (actual * target))


def forward_pass(queries, gate_mat, up_mat, down_mat):
    gate, up = rows_by(queries, [gate_mat, up_mat])
    _, act, _ = silu_parts(gate)
    out = three(nn, pair(act * up), pair(down_mat))
    return gate, up, out


def norm_sums(out, cotan, gain):
    return [jnp.sum(out * out, axis=1, keepdims=True), jnp.sum(gain * cotan * out, axis=1, keepdims=True)]


def forward_one_kernel(query_ref, cotan_ref, gain_ref, weights_ref, gate_ref, up_ref, out_ref, stats_ref):
    gate, up, out = forward_pass(query_ref[...], weights_ref[0], weights_ref[1], weights_ref[2])
    gate_ref[...] = gate
    up_ref[...] = up
    out_ref[...] = out
    stats_ref[...] = to_rows(norm_sums(out, cotan_ref[...].astype(f32), gain_ref[...]))


def forward_two_kernel(count, query_ref, cotan_ref, gain_ref, other_ref, *refs):
    chunks, (weights_ref, gate_ref, up_ref, out_ref, stats_ref) = refs[:count], refs[count:]
    piece = chunks[0].shape[1]
    for i, chunk in enumerate(chunks):
        weights_ref[:, i * piece : (i + 1) * piece, :] = chunk[...]
    gate, up, out = forward_pass(query_ref[...], weights_ref[0], weights_ref[1], weights_ref[2])
    gate_ref[...] = gate
    up_ref[...] = up
    out_ref[...] = out
    mine = to_rows([jnp.zeros((out.shape[0], 1), f32)] * 2 + norm_sums(out, cotan_ref[...].astype(f32), gain_ref[...]))
    stats_ref[...] = mine + other_ref[...]


def backward_kernel(first, width, count, query_ref, cotan_ref, gain_ref, stats_ref, weights_ref, gate_ref, up_ref, out_ref, grad_gate_ref, grad_up_ref, gain_term_ref, *parts_ref):
    columns = to_columns(stats_ref[...])
    square, product = columns[first], columns[first + 1]
    inverse = 1.0 / jnp.sqrt(square / width + EPSILON)
    out, cotan = out_ref[...], cotan_ref[...].astype(f32)
    grad_out = gain_ref[...] * cotan * inverse - out * (inverse * inverse * inverse * product / width)
    gain_term_ref[...] = jnp.sum(cotan * out * inverse, axis=0, keepdims=True)
    up = up_ref[...]
    _, act, slope = silu_parts(gate_ref[...])
    grad_out = pair(grad_out)
    back = three(nt, grad_out, pair(weights_ref[2]))
    grad_gate, grad_up = back * up * slope, back * act
    grad_gate_ref[...] = grad_gate
    grad_up_ref[...] = grad_up
    sum_gate, sum_up = sums_by([grad_gate, grad_up], query_ref[...])
    sum_down = three(tn, pair(act * up), grad_out)
    piece = sum_gate.shape[0] // count
    for i in range(count):
        at = slice(i * piece, (i + 1) * piece)
        parts_ref[i][0] = sum_gate[at]
        parts_ref[i][1] = sum_up[at]
        parts_ref[i][2] = sum_down[at]


def query_grad_kernel(grad_gate_ref, grad_up_ref, weights_ref, out_ref):
    total = three(nn, pair(grad_gate_ref[...]), pair(weights_ref[0]))
    total = total + three(nn, pair(grad_up_ref[...]), pair(weights_ref[1]))
    out_ref[...] = total.astype(bf16)


def second_order(keys, values, rate, weights, turns):
    gate, up, gate_turn, up_turn = rows_by(keys, [weights[0], weights[1], turns[0], turns[1]])
    back, back_turn = rows_by(values, [weights[2], turns[2]])
    back, back_turn = back * rate, back_turn * rate
    sig, act, slope = silu_parts(gate)
    bend = sig * (1.0 - sig) * (2.0 + gate * (1.0 - 2.0 * sig))
    hidden_turn = slope * gate_turn * up + act * up_turn
    cot_gate = back * (bend * gate_turn * up + slope * up_turn) + back_turn * up * slope
    cot_up = back * slope * gate_turn + back_turn * act
    return act * up, hidden_turn, cot_gate, cot_up, back * slope * up, back * act


def update_back_kernel(factor, key_ref, value_ref, rate_ref, weights_ref, turn_ref, gathered_ref, gain_ref, out_ref):
    keys, values = key_ref[...], value_ref[...]
    rate = minus_rate(rate_ref, factor)
    rows = weights_ref.shape[1]
    _, hidden_turn, cot_gate, cot_up, _, _ = second_order(keys, values, rate, [weights_ref[i] for i in range(3)], [turn_ref[i] for i in range(3)])
    sum_gate, sum_up = sums_by([cot_gate, cot_up], keys)
    (sum_down,) = sums_by([hidden_turn * rate], values)
    out_ref[0:rows] = sum_gate + gathered_ref[0]
    out_ref[rows : 2 * rows] = sum_up + gathered_ref[1]
    out_ref[2 * rows : 3 * rows] = sum_down + gathered_ref[2]
    out_ref[3 * rows :] = gain_ref[...]


def token_kernel(factor, key_ref, value_ref, rate_ref, weights_ref, *refs):
    turns_ref, (grad_key_ref, grad_value_ref, grad_rate_ref) = refs[:-3], refs[-3:]
    keys, values = key_ref[...], value_ref[...]
    rate = minus_rate(rate_ref, factor)
    weights = [weights_ref[i] for i in range(3)]
    turns = [jnp.concatenate([t[i] for t in turns_ref], axis=0) for i in range(3)]
    hidden, hidden_turn, cot_gate, cot_up, cot_gate_turn, cot_up_turn = second_order(keys, values, rate, weights, turns)
    grad_key = three(nn, pair(cot_gate), pair(weights[0])) + three(nn, pair(cot_up), pair(weights[1]))
    grad_key = grad_key + three(nn, pair(cot_gate_turn), pair(turns[0])) + three(nn, pair(cot_up_turn), pair(turns[1]))
    grad_key_ref[...] = grad_key.astype(bf16)
    grad_value = rate * (three(nn, pair(hidden_turn), pair(weights[2])) + three(nn, pair(hidden), pair(turns[2])))
    grad_value_ref[...] = grad_value.astype(bf16)
    grad_rate_ref[...] = to_rows([jnp.sum(grad_value * values.astype(f32), axis=1, keepdims=True)])[:1]


def call(kernel, outs, *args, scalars=0, name=None):
    in_specs = [pl.BlockSpec(memory_space=pltpu.SMEM)] * scalars + [pl.BlockSpec(memory_space=pltpu.VMEM)] * (len(args) - scalars)
    return pl.pallas_call(
        kernel,
        out_shape=[jax.ShapeDtypeStruct(shape, dtype) for shape, dtype in outs],
        in_specs=in_specs,
        out_specs=[pl.BlockSpec(memory_space=pltpu.VMEM)] * len(outs),
        compiler_params=pltpu.CompilerParams(vmem_limit_bytes=VMEM_BYTES),
        name=name,
    )(*args)


def local(chunks, heads, query_tokens, key_tokens, value_tokens, log_rate, fast_weights, norm_gain, out_grad):
    pairs, owner_table = ring_tables(chunks, heads)
    owner = jnp.asarray(owner_table)[lax.axis_index("head") % 2, lax.axis_index("ctx")]

    def send(x):
        return lax.ppermute(x, ("ctx", "head"), pairs)

    weights = fast_weights[0]
    query_one, query_two = query_tokens[0, :, 0, :], query_tokens[1, :, 0, :]
    cotan_one, cotan_two = out_grad[0, :, 0, :], out_grad[1, :, 0, :]
    keys, values = key_tokens[:, 0, :], value_tokens[:, 0, :]
    tokens, width = keys.shape
    hidden = weights.shape[1]
    rows = hidden // chunks
    piece = rows // SETS
    factor = (tokens * chunks * width) ** (-0.5)
    norm_width = heads * width
    token_f32, whole = ((tokens, width), f32), ((3, hidden, width), f32)
    small, chunk = ((3, piece, width), f32), ((3, rows, width), f32)
    hidden_f32 = ((tokens, hidden), f32)
    stats_shape = ((8, tokens), f32)

    def scatter(parts):
        totals = list(parts[0])
        for step in range(chunks - 1):
            totals = [send(t) for t in totals]
            if step < chunks - 2:
                totals = [t + p for t, p in zip(totals, parts[step + 1])]
        return totals

    def grid_of(flat):
        return [flat[i * SETS : (i + 1) * SETS] for i in range(chunks)]

    placed, *parts = call(
        partial(update_kernel, factor, chunks, SETS), [whole] + [small] * (chunks * SETS), owner, weights, keys, values, log_rate, scalars=1, name="update"
    )
    parts = grid_of(parts)
    arrived = scatter(parts)
    gate_one, up_one, out_one, stats_one = call(
        forward_one_kernel, [hidden_f32, hidden_f32, token_f32, stats_shape], query_one, cotan_one, norm_gain, placed, name="forward_one"
    )
    mine = placed[:, hidden - rows :, :]
    updates, news = [], []
    for i in range(SETS):
        update, new = call(renorm_kernel, [small, small], arrived[i], parts[-1][i], mine[:, i * piece : (i + 1) * piece, :], name="renorm")
        updates.append(update)
        news.append(new)
    gathered, held = [], list(news)
    for step in range(chunks - 1):
        held = [send(h) for h in held]
        gathered += held
    gathered += news

    new_weights, gate_two, up_two, out_two, stats = call(
        partial(forward_two_kernel, chunks * SETS),
        [whole, hidden_f32, hidden_f32, token_f32, stats_shape],
        query_two, cotan_two, norm_gain, stats_one, *gathered, name="forward_two",
    )
    stats = lax.psum(stats, "head")
    grad_gate, grad_up, gain_two, *parts = call(
        partial(backward_kernel, 2, norm_width, chunks * SETS), [hidden_f32, hidden_f32, ((1, width), f32)] + [small] * (chunks * SETS),
        query_two, cotan_two, norm_gain, stats, new_weights, gate_two, up_two, out_two, name="backward_two",
    )
    parts = grid_of(parts)
    arrived = scatter(parts)
    (grad_query_two,) = call(query_grad_kernel, [((tokens, width), bf16)], grad_gate, grad_up, new_weights, name="query_two")
    grad_gate, grad_up, gain_one, *direct_parts = call(
        partial(backward_kernel, 0, norm_width, chunks), [hidden_f32, hidden_f32, ((1, width), f32)] + [chunk] * chunks,
        query_one, cotan_one, norm_gain, stats, placed, gate_one, up_one, out_one, name="backward_one",
    )
    (grad_query_one,) = call(query_grad_kernel, [((tokens, width), bf16)], grad_gate, grad_up, placed, name="query_one")

    turn, direct = call(partial(renorm_back_kernel, SETS), [chunk, chunk], mine, *arrived, *parts[-1], *updates, name="renorm_back")
    gain_rows = (gain_one + gain_two).reshape(chunks, width // chunks)[owner]
    gain_rows = jnp.pad(gain_rows[:, None, :], ((0, 0), (0, 7), (0, width - width // chunks)))
    packed = ((3 * rows + 8, width), f32)

    def back_at(step, turned):
        (out,) = call(
            partial(update_back_kernel, factor), [packed], keys, values, log_rate, placed[:, step * rows : (step + 1) * rows, :], turned,
            direct_parts[step], gain_rows[step], name="update_back",
        )
        return out

    turns, total, held = [], None, turn
    for step in range(chunks - 1):
        held = send(held)
        turns.append(held)
        mine_now = back_at(step, held)
        total = send(mine_now if total is None else total + mine_now)
    turns.append(turn)
    grad_key, grad_value, grad_rate = call(
        partial(token_kernel, factor), [((tokens, width), bf16), ((tokens, width), bf16), ((1, tokens), f32)],
        keys, values, log_rate, placed, *turns, name="tokens",
    )
    total = total + back_at(chunks - 1, turn)
    grad_weights = total[: 3 * rows].reshape(3, rows, width) + direct
    grad_query = jnp.stack([grad_query_one, grad_query_two])[:, :, None, :]
    return (
        grad_query, grad_key[:, None, :], grad_value[:, None, :], grad_rate, grad_weights[None], total[3 * rows : 3 * rows + 1, : width // chunks],
    )


def solution(mesh):
    placed = (
        P(None, "ctx", "head", None),
        P("ctx", "head", None),
        P("ctx", "head", None),
        P("head", "ctx"),
        P("head", None, None, None),
        P("head", None),
        P(None, "ctx", "head", None),
    )
    return jax.shard_map(
        partial(local, mesh.shape["ctx"], mesh.shape["head"]),
        mesh=mesh,
        in_specs=placed,
        out_specs=(
            P(None, "ctx", "head", None),
            P("ctx", "head", None),
            P("ctx", "head", None),
            P("head", "ctx"),
            P("head", None, "ctx", None),
            P("head", "ctx"),
        ),
        check_vma=False,
    )
```

time: 468 us -> 270 us (0.58); the launches traced: 459 us -> 269 us
  waiting for transfers between devices: 345 us -> 98.9 us
  starting transfers between devices: 0.16 us -> 96.8 us
  matrix products: 58.4 us -> 0 us
  Pallas kernels: 0 us -> 37.8 us
  local copies, waits for them, and re-layouts: 6.94 us -> 25.3 us
  other arithmetic: 20.9 us -> 3.44 us
  between operations: 15.1 us -> 1.43 us
  blocking collectives: 12.9 us -> 5.73 us
    psum x2 -> x0, waiting for transfers between devices: 242 us -> none  [the longest x1 125 us: local(): total_grad = lax.psum(local_grad, 'ctx')]
    ppermute x0 -> x56, waiting for transfers between devices: none -> 98.9 us  [send(): return lax.ppermute(x, ('ctx', 'head'), pairs)]
    ppermute x0 -> x56, starting transfers between devices: none -> 96.8 us  [send(): return lax.ppermute(x, ('ctx', 'head'), pairs)]
    reduce_scatter x1 -> x0, waiting for transfers between devices: 63.9 us -> none  [local(): lax.psum_scatter(weight_one + weight_part, 'ctx', scatter_dimension=1, ti...]
    dot_general x36 -> x0, matrix products: 58.4 us -> none  [the longest x12 21.7 us: apply_fast(): jnp.dot(hidden, weights[2], precision=PRECISE, preferred_element_type=jnp...]
    unnamed x5 -> x0, waiting for transfers between devices: 39 us -> none
    pallas_call x0 -> x19, Pallas kernels: none -> 37.8 us  [call(): pl.pallas_call(kernel, out_shape=[jax.ShapeDtypeStruct(shape, dtype) for...]
    unnamed x110 -> x130, local copies, waits for them, and re-layouts: 6.86 us -> 21.7 us
  transfers between devices with their start and end apart: 4 -> 56, of which waited for: 4 -> 45; matrix products, arithmetic and copies ran while one was open for 11% -> 2% of each run, Pallas kernels for 0% -> 9%
where the time goes in v1:
time: 270 us; the launch traced here: 269 us
  waiting for transfers between devices  98.9 us (37%)
  starting transfers between devices  96.8 us (36%)
  Pallas kernels  37.8 us (14%)
  local copies, waits for them, and re-layouts  25.3 us (9%)
  blocking collectives  5.73 us (2%)
  other arithmetic  3.44 us (1%)
    ppermute x56, waiting for transfers between devices, send(): return lax.ppermute(x, ('ctx', 'head'), pairs)  98.9 us
    ppermute x56, starting transfers between devices, send(): return lax.ppermute(x, ('ctx', 'head'), pairs)  96.8 us
    pallas_call x19, Pallas kernels, call(): pl.pallas_call(kernel, out_shape=[jax.ShapeDtypeStruct(shape, dtype) for...  37.8 us
    unnamed x130, local copies, waits for them, and re-layouts  21.7 us
    psum x1, blocking collectives, local(): stats = lax.psum(stats, 'head')  5.73 us
  transfers between devices with their start and end apart: 56, of which 45 were waited for; matrix products, arithmetic and copies ran while one was open for 2% of the time, Pallas kernels for 9%

profile of v1, /device:TPU:0, one launch (start us, length us, event | category | flops | bytes accessed | tf_op | source)
XLA Modules:
  0.0 269.4 jit_solution(6263860697244710419)
XLA Ops:
  3.9 5.9 %update.1 = (f32[3,512,512]{2,1,0:T(8,128)}, f32[3,32,512]{2,1,0:T(8,128)S(1)}, f32[3,32,512]{2,1,0:T(8,128)S(1)}, f32[3,32,512]{2,1,0:T(8,128)S(1)}, f32[3,32,5...) custom-call(s32[8]{0:T(128)S(1)} %fusion.9.owner_ref, ...), custom_call_target="tpu_custom_call" | custom-call | tf_op jit(solution)/shard_map/update/pallas_call | solution.py:271
  9.8 2.9 %collective-permute-start = (f32[3,32,512]{2,1,0:T(8,128)S(1)}, f32[3,32,512]{2,1,0:T(8,128)S(1)}, u32[]{:S(2)}, u32[]{:S(2)}) collective-permute-start(f32[3,32,512]{2,1,0:T(8,128)S(1)} %get-tuple-element.73), channel_id=1, source_target_pairs={{0,4},{4,12},{12,20},{20,28},{28,24},{24,16},{16,8},{8,0},{9,17},{... | collective-permute-start | bytes 589832 | tf_op jit(solution)/shard_map/ppermute | solution.py:286
  14.3 2.2 collective-permute-done
  16.5 2.0 collective-permute-start.1
  18.6 2.0 collective-permute-start.9
  22.3 2.0 collective-permute-start.2
  24.4 2.0 collective-permute-start.10
  28.1 2.0 collective-permute-start.3
  30.1 2.0 collective-permute-start.11
  32.1 1.7 collective-permute-done.3
  33.8 2.0 collective-permute-start.4
  35.9 2.0 collective-permute-start.12
  39.6 2.0 collective-permute-start.5
  41.7 2.0 collective-permute-start.13
  45.3 2.0 collective-permute-start.6
  47.4 2.0 collective-permute-start.14
  51.9 1.9 collective-permute-start.7
  57.6 1.9 collective-permute-start.16
  63.2 1.9 collective-permute-start.18
  68.9 1.9 collective-permute-start.20
  74.6 1.9 collective-permute-start.22
  80.2 1.9 collective-permute-start.24
  85.9 1.9 collective-permute-start.26
  95.0 3.2 %forward_two.1 = (f32[3,512,512]{2,1,0:T(8,128)}, f32[256,512]{1,0:T(8,128)S(1)}, f32[256,512]{1,0:T(8,128)S(1)}, f32[256,512]{1,0:T(8,128)S(1)}, f32[8,256]{1,0:T(8,128)S(1)}) custom-call(bf16[256,512]{1,0:T(8,128)(2,1)S(1)} %get-tuple-element.164.query_ref, bf16[256,512]{1,0:T(8,128)(2,1)S(1)} %get-tuple-element.153.cotan_ref, f32[1,512]{1,0:T(1,128)S(1)} %copy-done.62, ...), custom_call_target="tpu_custom_call" | custom-call | tf_op jit(solution)/shard_map/forward_two/pallas_call | solution.py:271
  100.6 5.7 %psum.7.stats_ref = f32[8,256]{1,0:T(8,128)S(1)} all-reduce(f32[8,256]{1,0:T(8,128)S(1)} %get-tuple-element.91), channel_id=1, replica_groups=mesh['ctx'=8,'head'=4] {'head'}, use_global_device_ids=true, to_apply=%region_0.1 | all-reduce | flops 2048 | bytes 16384 | tf_op jit(solution)/shard_map/psum | solution.py:339
  109.4 4.3 %backward_two.1 = (f32[256,512]{1,0:T(8,128)S(1)}, f32[256,512]{1,0:T(8,128)S(1)}, f32[1,512]{1,0:T(1,128)S(1)}, f32[3,32,512]{2,1,0:T(8,128)S(1)}, f32[3,32,512...) custom-call(bf16[256,512]{1,0:T(8,128)(2,1)S(1)} %copy-done.12, ...), custom_call_target="tpu_custom_call" | custom-call | tf_op jit(solution)/shard_map/backward_two/pallas_call | solution.py:271
  116.9 2.5 collective-permute-done.28
  123.2 2.0 collective-permute-done.29
  125.2 1.6 collective-permute-start.30
  129.0 2.0 collective-permute-done.30
  131.0 1.6 collective-permute-start.31
  134.7 2.0 collective-permute-done.31
  136.7 1.6 collective-permute-start.32
  140.5 2.0 collective-permute-done.32
  142.5 1.8 collective-permute-start.33
  144.6 1.6 collective-permute-start.40
  146.2 2.2 collective-permute-done.33
  148.4 1.6 collective-permute-start.34
  154.2 2.1 collective-permute-done.41.refs_1_
  159.0 4.3 %backward_one.1 = (f32[256,512]{1,0:T(8,128)S(1)}, f32[256,512]{1,0:T(8,128)S(1)}, f32[1,512]{1,0:T(1,128)S(1)}, f32[3,64,512]{2,1,0:T(8,128)S(1)}, f32[3,64,512...) custom-call(bf16[256,512]{1,0:T(8,128)(2,1)S(1)} %copy-done.10, ...), custom_call_target="tpu_custom_call" | custom-call | tf_op jit(solution)/shard_map/backward_one/pallas_call | solution.py:271
  176.0 9.3 %collective-permute-done.43.refs_1_.turn_ref = f32[3,64,512]{2,1,0:T(8,128)S(1)} collective-permute-done((f32[3,64,512]{2,1,0:T(8,128)S(1)}, f32[3,64,512]{2,1,0:T(8,128)S(1)}, u32[]{:S(2)}, u32[]{:S(2)}) %collective-permute-start.43) | collective-permute-done | bytes 393248 | tf_op jit(solution)/shard_map/ppermute | solution.py:286
  190.4 9.3 %collective-permute-done.44.refs_2_.turn_ref = f32[3,64,512]{2,1,0:T(8,128)S(1)} collective-permute-done((f32[3,64,512]{2,1,0:T(8,128)S(1)}, f32[3,64,512]{2,1,0:T(8,128)S(1)}, u32[]{:S(2)}, u32[]{:S(2)}) %collective-permute-start.44) | collective-permute-done | bytes 393248 | tf_op jit(solution)/shard_map/ppermute | solution.py:286
  203.8 9.3 %collective-permute-done.45.refs_3_.turn_ref = f32[3,64,512]{2,1,0:T(8,128)S(1)} collective-permute-done((f32[3,64,512]{2,1,0:T(8,128)S(1)}, f32[3,64,512]{2,1,0:T(8,128)S(1)}, u32[]{:S(2)}, u32[]{:S(2)}) %collective-permute-start.45) | collective-permute-done | bytes 393248 | tf_op jit(solution)/shard_map/ppermute | solution.py:286
  217.2 9.3 %collective-permute-done.46.refs_4_.turn_ref = f32[3,64,512]{2,1,0:T(8,128)S(1)} collective-permute-done((f32[3,64,512]{2,1,0:T(8,128)S(1)}, f32[3,64,512]{2,1,0:T(8,128)S(1)}, u32[]{:S(2)}, u32[]{:S(2)}) %collective-permute-start.46) | collective-permute-done | bytes 393248 | tf_op jit(solution)/shard_map/ppermute | solution.py:286
  230.6 9.3 %collective-permute-done.47.refs_5_.turn_ref = f32[3,64,512]{2,1,0:T(8,128)S(1)} collective-permute-done((f32[3,64,512]{2,1,0:T(8,128)S(1)}, f32[3,64,512]{2,1,0:T(8,128)S(1)}, u32[]{:S(2)}, u32[]{:S(2)}) %collective-permute-start.47) | collective-permute-done | bytes 393248 | tf_op jit(solution)/shard_map/ppermute | solution.py:286
  244.0 9.3 %collective-permute-done.48.refs_6_.turn_ref = f32[3,64,512]{2,1,0:T(8,128)S(1)} collective-permute-done((f32[3,64,512]{2,1,0:T(8,128)S(1)}, f32[3,64,512]{2,1,0:T(8,128)S(1)}, u32[]{:S(2)}, u32[]{:S(2)}) %collective-permute-start.48) | collective-permute-done | bytes 393248 | tf_op jit(solution)/shard_map/ppermute | solution.py:286
  254.5 1.9 collective-permute-start.55
  260.4 7.5 %tokens.1 = (bf16[256,512]{1,0:T(8,128)(2,1)}, bf16[256,512]{1,0:T(8,128)(2,1)}, f32[1,256]{1,0:T(1,128)}) custom-call(bf16[256,512]{1,0:T(8,128)(2,1)S(1)} %bitcast.54, bf16[256,512]{1,0:T(8,128)(2,1)S(1)} %bitcast.64, f32[1,256]{1,0:T(1,128)S(1)} %copy-done.61, f32[3,512,512]{2,1,0:T(8,128)} %get-tuple-element.71.weights_ref, ...), custom_call_target="tpu_custom_call" | custom-call | tf_op jit(solution)/shard_map/tokens/pallas_call | solution.py:271
  (259 shorter events, 110.4 us)
Async XLA Ops:
  9.8 6.7 %collective-permute-start = (f32[3,32,512]{2,1,0:T(8,128)S(1)}, f32[3,32,512]{2,1,0:T(8,128)S(1)}, u32[]{:S(2)}, u32[]{:S(2)}) collective-permute-start(f32[3,32,512]{2,1,0:T(8,128)S(1)} %get-tuple-element.73), channel_id=1, source_target_pairs={{0,4},{4,12},{12,20},{20,28},{28,24},{24,16},{16,8},{8,0},{9,17},{... | collective-permute-start | bytes 589832 | tf_op jit(solution)/shard_map/ppermute | solution.py:286
  12.8 5.8 %collective-permute-start.8 = (f32[3,32,512]{2,1,0:T(8,128)S(1)}, f32[3,32,512]{2,1,0:T(8,128)S(1)}, u32[]{:S(2)}, u32[]{:S(2)}) collective-permute-start(f32[3,32,512]{2,1,0:T(8,128)S(1)} %get-tuple-element.82), channel_id=1, source_target_pairs={{0,4},{4,12},{12,20},{20,28},{28,24},{24,16},{16,8},{8,0},{9,17},{... | collective-permute-start | bytes 589832 | tf_op jit(solution)/shard_map/ppermute | solution.py:286
  16.5 5.7 %collective-permute-start.1 = (f32[3,32,512]{2,1,0:T(8,128)S(1)}, f32[3,32,512]{2,1,0:T(8,128)S(1)}, u32[]{:S(2)}, u32[]{:S(2)}) collective-permute-start(f32[3,32,512]{2,1,0:T(8,128)S(1)} %add.126), channel_id=1, source_target_pairs={{0,4},{4,12},{12,20},{20,28},{28,24},{24,16},{16,8},{8,0},{9,17},{... | collective-permute-start | bytes 589832 | tf_op jit(solution)/shard_map/ppermute | solution.py:286
  18.6 5.7 %collective-permute-start.9 = (f32[3,32,512]{2,1,0:T(8,128)S(1)}, f32[3,32,512]{2,1,0:T(8,128)S(1)}, u32[]{:S(2)}, u32[]{:S(2)}) collective-permute-start(f32[3,32,512]{2,1,0:T(8,128)S(1)} %add.132), channel_id=1, source_target_pairs={{0,4},{4,12},{12,20},{20,28},{28,24},{24,16},{16,8},{8,0},{9,17},{... | collective-permute-start | bytes 589832 | tf_op jit(solution)/shard_map/ppermute | solution.py:286
  22.3 5.7 %collective-permute-start.2 = (f32[3,32,512]{2,1,0:T(8,128)S(1)}, f32[3,32,512]{2,1,0:T(8,128)S(1)}, u32[]{:S(2)}, u32[]{:S(2)}) collective-permute-start(f32[3,32,512]{2,1,0:T(8,128)S(1)} %add.127), channel_id=1, source_target_pairs={{0,4},{4,12},{12,20},{20,28},{28,24},{24,16},{16,8},{8,0},{9,17},{... | collective-permute-start | bytes 589832 | tf_op jit(solution)/shard_map/ppermute | solution.py:286
  24.4 5.7 %collective-permute-start.10 = (f32[3,32,512]{2,1,0:T(8,128)S(1)}, f32[3,32,512]{2,1,0:T(8,128)S(1)}, u32[]{:S(2)}, u32[]{:S(2)}) collective-permute-start(f32[3,32,512]{2,1,0:T(8,128)S(1)} %add.133), channel_id=1, source_target_pairs={{0,4},{4,12},{12,20},{20,28},{28,24},{24,16},{16,8},{8,0},{9,17},{... | collective-permute-start | bytes 589832 | tf_op jit(solution)/shard_map/ppermute | solution.py:286
  28.1 5.7 %collective-permute-start.3 = (f32[3,32,512]{2,1,0:T(8,128)S(1)}, f32[3,32,512]{2,1,0:T(8,128)S(1)}, u32[]{:S(2)}, u32[]{:S(2)}) collective-permute-start(f32[3,32,512]{2,1,0:T(8,128)S(1)} %add.128), channel_id=1, source_target_pairs={{0,4},{4,12},{12,20},{20,28},{28,24},{24,16},{16,8},{8,0},{9,17},{... | collective-permute-start | bytes 589832 | tf_op jit(solution)/shard_map/ppermute | solution.py:286
  30.1 5.7 %collective-permute-start.11 = (f32[3,32,512]{2,1,0:T(8,128)S(1)}, f32[3,32,512]{2,1,0:T(8,128)S(1)}, u32[]{:S(2)}, u32[]{:S(2)}) collective-permute-start(f32[3,32,512]{2,1,0:T(8,128)S(1)} %add.134), channel_id=1, source_target_pairs={{0,4},{4,12},{12,20},{20,28},{28,24},{24,16},{16,8},{8,0},{9,17},{... | collective-permute-start | bytes 589832 | tf_op jit(solution)/shard_map/ppermute | solution.py:286
  33.8 5.7 %collective-permute-start.4 = (f32[3,32,512]{2,1,0:T(8,128)S(1)}, f32[3,32,512]{2,1,0:T(8,128)S(1)}, u32[]{:S(2)}, u32[]{:S(2)}) collective-permute-start(f32[3,32,512]{2,1,0:T(8,128)S(1)} %add.129), channel_id=1, source_target_pairs={{0,4},{4,12},{12,20},{20,28},{28,24},{24,16},{16,8},{8,0},{9,17},{... | collective-permute-start | bytes 589832 | tf_op jit(solution)/shard_map/ppermute | solution.py:286
  35.9 5.7 %collective-permute-start.12 = (f32[3,32,512]{2,1,0:T(8,128)S(1)}, f32[3,32,512]{2,1,0:T(8,128)S(1)}, u32[]{:S(2)}, u32[]{:S(2)}) collective-permute-start(f32[3,32,512]{2,1,0:T(8,128)S(1)} %add.135), channel_id=1, source_target_pairs={{0,4},{4,12},{12,20},{20,28},{28,24},{24,16},{16,8},{8,0},{9,17},{... | collective-permute-start | bytes 589832 | tf_op jit(solution)/shard_map/ppermute | solution.py:286
  39.6 5.7 %collective-permute-start.5 = (f32[3,32,512]{2,1,0:T(8,128)S(1)}, f32[3,32,512]{2,1,0:T(8,128)S(1)}, u32[]{:S(2)}, u32[]{:S(2)}) collective-permute-start(f32[3,32,512]{2,1,0:T(8,128)S(1)} %add.130), channel_id=1, source_target_pairs={{0,4},{4,12},{12,20},{20,28},{28,24},{24,16},{16,8},{8,0},{9,17},{... | collective-permute-start | bytes 589832 | tf_op jit(solution)/shard_map/ppermute | solution.py:286
  41.7 5.7 %collective-permute-start.13 = (f32[3,32,512]{2,1,0:T(8,128)S(1)}, f32[3,32,512]{2,1,0:T(8,128)S(1)}, u32[]{:S(2)}, u32[]{:S(2)}) collective-permute-start(f32[3,32,512]{2,1,0:T(8,128)S(1)} %add.136), channel_id=1, source_target_pairs={{0,4},{4,12},{12,20},{20,28},{28,24},{24,16},{16,8},{8,0},{9,17},{... | collective-permute-start | bytes 589832 | tf_op jit(solution)/shard_map/ppermute | solution.py:286
  45.3 5.7 %collective-permute-start.6 = (f32[3,32,512]{2,1,0:T(8,128)S(1)}, f32[3,32,512]{2,1,0:T(8,128)S(1)}, u32[]{:S(2)}, u32[]{:S(2)}) collective-permute-start(f32[3,32,512]{2,1,0:T(8,128)S(1)} %add.131), channel_id=1, source_target_pairs={{0,4},{4,12},{12,20},{20,28},{28,24},{24,16},{16,8},{8,0},{9,17},{... | collective-permute-start | bytes 589832 | tf_op jit(solution)/shard_map/ppermute | solution.py:286
  47.4 6.4 %collective-permute-start.14 = (f32[3,32,512]{2,1,0:T(8,128)S(1)}, f32[3,32,512]{2,1,0:T(8,128)S(1)}, u32[]{:S(2)}, u32[]{:S(2)}) collective-permute-start(f32[3,32,512]{2,1,0:T(8,128)S(1)} %add.137), channel_id=1, source_target_pairs={{0,4},{4,12},{12,20},{20,28},{28,24},{24,16},{16,8},{8,0},{9,17},{... | collective-permute-start | bytes 589832 | tf_op jit(solution)/shard_map/ppermute | solution.py:286
  51.9 5.7 %collective-permute-start.7 = (f32[3,32,512]{2,1,0:T(8,128)S(1)}, f32[3,32,512]{2,1,0:T(8,128)S(1)}, u32[]{:S(2)}, u32[]{:S(2)}) collective-permute-start(f32[3,32,512]{2,1,0:T(8,128)S(1)} %get-tuple-element.81.refs_14_), channel_id=1, source_target_pairs={{0,4},{4,12},{12,20},{20,28},{28,24},{24,16},{16,8},{8,0},{9,17},{... | collective-permute-start | bytes 589832 | tf_op jit(solution)/shard_map/ppermute | solution.py:286
  54.7 5.7 %collective-permute-start.15 = (f32[3,32,512]{2,1,0:T(8,128)S(1)}, f32[3,32,512]{2,1,0:T(8,128)S(1)}, u32[]{:S(2)}, u32[]{:S(2)}) collective-permute-start(f32[3,32,512]{2,1,0:T(8,128)S(1)} %get-tuple-element.90.refs_15_), channel_id=1, source_target_pairs={{0,4},{4,12},{12,20},{20,28},{28,24},{24,16},{16,8},{8,0},{9,17},{... | collective-permute-start | bytes 589832 | tf_op jit(solution)/shard_map/ppermute | solution.py:286
  57.6 5.7 %collective-permute-start.16 = (f32[3,32,512]{2,1,0:T(8,128)S(1)}, f32[3,32,512]{2,1,0:T(8,128)S(1)}, u32[]{:S(2)}, u32[]{:S(2)}) collective-permute-start(f32[3,32,512]{2,1,0:T(8,128)S(1)} %collective-permute-done.7.refs_0_), channel_id=1, source_target_pairs={{0,4},{4,12},{12,20},{20,28},{28,24},{24,16},{16,8},{8,0},{9,17},{... | collective-permute-start | bytes 589832 | tf_op jit(solution)/shard_map/ppermute | solution.py:286
  60.3 5.7 %collective-permute-start.17 = (f32[3,32,512]{2,1,0:T(8,128)S(1)}, f32[3,32,512]{2,1,0:T(8,128)S(1)}, u32[]{:S(2)}, u32[]{:S(2)}) collective-permute-start(f32[3,32,512]{2,1,0:T(8,128)S(1)} %collective-permute-done.15.refs_1_), channel_id=1, source_target_pairs={{0,4},{4,12},{12,20},{20,28},{28,24},{24,16},{16,8},{8,0},{9,17},{... | collective-permute-start | bytes 589832 | tf_op jit(solution)/shard_map/ppermute | solution.py:286
  85.9 9.1 %collective-permute-start.26 = (f32[3,32,512]{2,1,0:T(8,128)S(1)}, f32[3,32,512]{2,1,0:T(8,128)S(1)}, u32[]{:S(2)}, u32[]{:S(2)}) collective-permute-start(f32[3,32,512]{2,1,0:T(8,128)S(1)} %collective-permute-done.24.refs_10_), channel_id=1, source_target_pairs={{0,4},{4,12},{12,20},{20,28},{28,24},{24,16},{16,8},{8,0},{9,17},{... | collective-permute-start | bytes 589832 | tf_op jit(solution)/shard_map/ppermute | solution.py:286
  88.7 6.4 %collective-permute-start.27 = (f32[3,32,512]{2,1,0:T(8,128)S(1)}, f32[3,32,512]{2,1,0:T(8,128)S(1)}, u32[]{:S(2)}, u32[]{:S(2)}) collective-permute-start(f32[3,32,512]{2,1,0:T(8,128)S(1)} %collective-permute-done.25.refs_11_), channel_id=1, source_target_pairs={{0,4},{4,12},{12,20},{20,28},{28,24},{24,16},{16,8},{8,0},{9,17},{... | collective-permute-start | bytes 589832 | tf_op jit(solution)/shard_map/ppermute | solution.py:286
  113.7 5.7 %collective-permute-start.28 = (f32[3,32,512]{2,1,0:T(8,128)S(1)}, f32[3,32,512]{2,1,0:T(8,128)S(1)}, u32[]{:S(2)}, u32[]{:S(2)}) collective-permute-start(f32[3,32,512]{2,1,0:T(8,128)S(1)} %get-tuple-element.103), channel_id=1, source_target_pairs={{0,4},{4,12},{12,20},{20,28},{28,24},{24,16},{16,8},{8,0},{9,17},{... | collective-permute-start | bytes 589832 | tf_op jit(solution)/shard_map/ppermute | solution.py:286
  115.4 6.2 %collective-permute-start.35 = (f32[3,32,512]{2,1,0:T(8,128)S(1)}, f32[3,32,512]{2,1,0:T(8,128)S(1)}, u32[]{:S(2)}, u32[]{:S(2)}) collective-permute-start(f32[3,32,512]{2,1,0:T(8,128)S(1)} %get-tuple-element.110), channel_id=1, source_target_pairs={{0,4},{4,12},{12,20},{20,28},{28,24},{24,16},{16,8},{8,0},{9,17},{... | collective-permute-start | bytes 589832 | tf_op jit(solution)/shard_map/ppermute | solution.py:286
  119.5 5.7 %collective-permute-start.29 = (f32[3,32,512]{2,1,0:T(8,128)S(1)}, f32[3,32,512]{2,1,0:T(8,128)S(1)}, u32[]{:S(2)}, u32[]{:S(2)}) collective-permute-start(f32[3,32,512]{2,1,0:T(8,128)S(1)} %add.138), channel_id=1, source_target_pairs={{0,4},{4,12},{12,20},{20,28},{28,24},{24,16},{16,8},{8,0},{9,17},{... | collective-permute-start | bytes 589832 | tf_op jit(solution)/shard_map/ppermute | solution.py:286
  121.6 5.7 %collective-permute-start.36 = (f32[3,32,512]{2,1,0:T(8,128)S(1)}, f32[3,32,512]{2,1,0:T(8,128)S(1)}, u32[]{:S(2)}, u32[]{:S(2)}) collective-permute-start(f32[3,32,512]{2,1,0:T(8,128)S(1)} %add.144), channel_id=1, source_target_pairs={{0,4},{4,12},{12,20},{20,28},{28,24},{24,16},{16,8},{8,0},{9,17},{... | collective-permute-start | bytes 589832 | tf_op jit(solution)/shard_map/ppermute | solution.py:286
  125.2 5.7 %collective-permute-start.30 = (f32[3,32,512]{2,1,0:T(8,128)S(1)}, f32[3,32,512]{2,1,0:T(8,128)S(1)}, u32[]{:S(2)}, u32[]{:S(2)}) collective-permute-start(f32[3,32,512]{2,1,0:T(8,128)S(1)} %add.139), channel_id=1, source_target_pairs={{0,4},{4,12},{12,20},{20,28},{28,24},{24,16},{16,8},{8,0},{9,17},{... | collective-permute-start | bytes 589832 | tf_op jit(solution)/shard_map/ppermute | solution.py:286
  127.3 5.7 %collective-permute-start.37 = (f32[3,32,512]{2,1,0:T(8,128)S(1)}, f32[3,32,512]{2,1,0:T(8,128)S(1)}, u32[]{:S(2)}, u32[]{:S(2)}) collective-permute-start(f32[3,32,512]{2,1,0:T(8,128)S(1)} %add.145), channel_id=1, source_target_pairs={{0,4},{4,12},{12,20},{20,28},{28,24},{24,16},{16,8},{8,0},{9,17},{... | collective-permute-start | bytes 589832 | tf_op jit(solution)/shard_map/ppermute | solution.py:286
  131.0 5.7 %collective-permute-start.31 = (f32[3,32,512]{2,1,0:T(8,128)S(1)}, f32[3,32,512]{2,1,0:T(8,128)S(1)}, u32[]{:S(2)}, u32[]{:S(2)}) collective-permute-start(f32[3,32,512]{2,1,0:T(8,128)S(1)} %add.140), channel_id=1, source_target_pairs={{0,4},{4,12},{12,20},{20,28},{28,24},{24,16},{16,8},{8,0},{9,17},{... | collective-permute-start | bytes 589832 | tf_op jit(solution)/shard_map/ppermute | solution.py:286
  133.1 5.7 %collective-permute-start.38 = (f32[3,32,512]{2,1,0:T(8,128)S(1)}, f32[3,32,512]{2,1,0:T(8,128)S(1)}, u32[]{:S(2)}, u32[]{:S(2)}) collective-permute-start(f32[3,32,512]{2,1,0:T(8,128)S(1)} %add.146), channel_id=1, source_target_pairs={{0,4},{4,12},{12,20},{20,28},{28,24},{24,16},{16,8},{8,0},{9,17},{... | collective-permute-start | bytes 589832 | tf_op jit(solution)/shard_map/ppermute | solution.py:286
  136.7 5.7 %collective-permute-start.32 = (f32[3,32,512]{2,1,0:T(8,128)S(1)}, f32[3,32,512]{2,1,0:T(8,128)S(1)}, u32[]{:S(2)}, u32[]{:S(2)}) collective-permute-start(f32[3,32,512]{2,1,0:T(8,128)S(1)} %add.141), channel_id=1, source_target_pairs={{0,4},{4,12},{12,20},{20,28},{28,24},{24,16},{16,8},{8,0},{9,17},{... | collective-permute-start | bytes 589832 | tf_op jit(solution)/shard_map/ppermute | solution.py:286
  138.8 5.7 %collective-permute-start.39 = (f32[3,32,512]{2,1,0:T(8,128)S(1)}, f32[3,32,512]{2,1,0:T(8,128)S(1)}, u32[]{:S(2)}, u32[]{:S(2)}) collective-permute-start(f32[3,32,512]{2,1,0:T(8,128)S(1)} %add.147), channel_id=1, source_target_pairs={{0,4},{4,12},{12,20},{20,28},{28,24},{24,16},{16,8},{8,0},{9,17},{... | collective-permute-start | bytes 589832 | tf_op jit(solution)/shard_map/ppermute | solution.py:286
  142.5 5.9 %collective-permute-start.33 = (f32[3,32,512]{2,1,0:T(8,128)S(1)}, f32[3,32,512]{2,1,0:T(8,128)S(1)}, u32[]{:S(2)}, u32[]{:S(2)}) collective-permute-start(f32[3,32,512]{2,1,0:T(8,128)S(1)} %add.142), channel_id=1, source_target_pairs={{0,4},{4,12},{12,20},{20,28},{28,24},{24,16},{16,8},{8,0},{9,17},{... | collective-permute-start | bytes 589832 | tf_op jit(solution)/shard_map/ppermute | solution.py:286
  144.6 5.9 %collective-permute-start.40 = (f32[3,32,512]{2,1,0:T(8,128)S(1)}, f32[3,32,512]{2,1,0:T(8,128)S(1)}, u32[]{:S(2)}, u32[]{:S(2)}) collective-permute-start(f32[3,32,512]{2,1,0:T(8,128)S(1)} %add.148), channel_id=1, source_target_pairs={{0,4},{4,12},{12,20},{20,28},{28,24},{24,16},{16,8},{8,0},{9,17},{... | collective-permute-start | bytes 589832 | tf_op jit(solution)/shard_map/ppermute | solution.py:286
  148.4 5.7 %collective-permute-start.34 = (f32[3,32,512]{2,1,0:T(8,128)S(1)}, f32[3,32,512]{2,1,0:T(8,128)S(1)}, u32[]{:S(2)}, u32[]{:S(2)}) collective-permute-start(f32[3,32,512]{2,1,0:T(8,128)S(1)} %add.143), channel_id=1, source_target_pairs={{0,4},{4,12},{12,20},{20,28},{28,24},{24,16},{16,8},{8,0},{9,17},{... | collective-permute-start | bytes 589832 | tf_op jit(solution)/shard_map/ppermute | solution.py:286
  150.6 5.7 %collective-permute-start.41 = (f32[3,32,512]{2,1,0:T(8,128)S(1)}, f32[3,32,512]{2,1,0:T(8,128)S(1)}, u32[]{:S(2)}, u32[]{:S(2)}) collective-permute-start(f32[3,32,512]{2,1,0:T(8,128)S(1)} %add.149), channel_id=1, source_target_pairs={{0,4},{4,12},{12,20},{20,28},{28,24},{24,16},{16,8},{8,0},{9,17},{... | collective-permute-start | bytes 589832 | tf_op jit(solution)/shard_map/ppermute | solution.py:286
  156.7 14.3 %collective-permute-start.42 = (f32[3,64,512]{2,1,0:T(8,128)S(1)}, f32[3,64,512]{2,1,0:T(8,128)S(1)}, u32[]{:S(2)}, u32[]{:S(2)}) collective-permute-start(f32[3,64,512]{2,1,0:T(8,128)S(1)} %get-tuple-element.121.refs_7_.turn_ref), channel_id=1, source_target_pairs={{0,4},{4,12},{12,20},{20,28},{28,24},{24,16},{16,8},{8,0},{9,17},{... | collective-permute-start | bytes 1179656 | tf_op jit(solution)/shard_map/ppermute | solution.py:286
  173.1 14.3 %collective-permute-start.49 = (f32[200,512]{1,0:T(8,128)S(1)}, f32[200,512]{1,0:T(8,128)S(1)}, u32[]{:S(2)}, u32[]{:S(2)}) collective-permute-start(f32[200,512]{1,0:T(8,128)S(1)} %update_back.8), channel_id=1, source_target_pairs={{0,4},{4,12},{12,20},{20,28},{28,24},{24,16},{16,8},{8,0},{9,17},{... | collective-permute-start | bytes 1228808 | tf_op jit(solution)/shard_map/ppermute | solution.py:286
  174.8 10.6 %collective-permute-start.43 = (f32[3,64,512]{2,1,0:T(8,128)S(1)}, f32[3,64,512]{2,1,0:T(8,128)S(1)}, u32[]{:S(2)}, u32[]{:S(2)}) collective-permute-start(f32[3,64,512]{2,1,0:T(8,128)S(1)} %collective-permute-done.42.refs_0_.turn_ref), channel_id=1, source_target_pairs={{0,4},{4,12},{12,20},{20,28},{28,24},{24,16},{16,8},{8,0},{9,17},{... | collective-permute-start | bytes 1179656 | tf_op jit(solution)/shard_map/ppermute | solution.py:286
  187.5 13.3 %collective-permute-start.50 = (f32[200,512]{1,0:T(8,128)S(1)}, f32[200,512]{1,0:T(8,128)S(1)}, u32[]{:S(2)}, u32[]{:S(2)}) collective-permute-start(f32[200,512]{1,0:T(8,128)S(1)} %add.152), channel_id=1, source_target_pairs={{0,4},{4,12},{12,20},{20,28},{28,24},{24,16},{16,8},{8,0},{9,17},{... | collective-permute-start | bytes 1228808 | tf_op jit(solution)/shard_map/ppermute | solution.py:286
  189.1 10.6 %collective-permute-start.44 = (f32[3,64,512]{2,1,0:T(8,128)S(1)}, f32[3,64,512]{2,1,0:T(8,128)S(1)}, u32[]{:S(2)}, u32[]{:S(2)}) collective-permute-start(f32[3,64,512]{2,1,0:T(8,128)S(1)} %collective-permute-done.43.refs_1_.turn_ref), channel_id=1, source_target_pairs={{0,4},{4,12},{12,20},{20,28},{28,24},{24,16},{16,8},{8,0},{9,17},{... | collective-permute-start | bytes 1179656 | tf_op jit(solution)/shard_map/ppermute | solution.py:286
  200.9 13.3 %collective-permute-start.51 = (f32[200,512]{1,0:T(8,128)S(1)}, f32[200,512]{1,0:T(8,128)S(1)}, u32[]{:S(2)}, u32[]{:S(2)}) collective-permute-start(f32[200,512]{1,0:T(8,128)S(1)} %add.153), channel_id=1, source_target_pairs={{0,4},{4,12},{12,20},{20,28},{28,24},{24,16},{16,8},{8,0},{9,17},{... | collective-permute-start | bytes 1228808 | tf_op jit(solution)/shard_map/ppermute | solution.py:286
  202.5 10.6 %collective-permute-start.45 = (f32[3,64,512]{2,1,0:T(8,128)S(1)}, f32[3,64,512]{2,1,0:T(8,128)S(1)}, u32[]{:S(2)}, u32[]{:S(2)}) collective-permute-start(f32[3,64,512]{2,1,0:T(8,128)S(1)} %collective-permute-done.44.refs_2_.turn_ref), channel_id=1, source_target_pairs={{0,4},{4,12},{12,20},{20,28},{28,24},{24,16},{16,8},{8,0},{9,17},{... | collective-permute-start | bytes 1179656 | tf_op jit(solution)/shard_map/ppermute | solution.py:286
  214.3 13.3 %collective-permute-start.52 = (f32[200,512]{1,0:T(8,128)S(1)}, f32[200,512]{1,0:T(8,128)S(1)}, u32[]{:S(2)}, u32[]{:S(2)}) collective-permute-start(f32[200,512]{1,0:T(8,128)S(1)} %add.154), channel_id=1, source_target_pairs={{0,4},{4,12},{12,20},{20,28},{28,24},{24,16},{16,8},{8,0},{9,17},{... | collective-permute-start | bytes 1228808 | tf_op jit(solution)/shard_map/ppermute | solution.py:286
  215.9 10.6 %collective-permute-start.46 = (f32[3,64,512]{2,1,0:T(8,128)S(1)}, f32[3,64,512]{2,1,0:T(8,128)S(1)}, u32[]{:S(2)}, u32[]{:S(2)}) collective-permute-start(f32[3,64,512]{2,1,0:T(8,128)S(1)} %collective-permute-done.45.refs_3_.turn_ref), channel_id=1, source_target_pairs={{0,4},{4,12},{12,20},{20,28},{28,24},{24,16},{16,8},{8,0},{9,17},{... | collective-permute-start | bytes 1179656 | tf_op jit(solution)/shard_map/ppermute | solution.py:286
  227.7 13.3 %collective-permute-start.53 = (f32[200,512]{1,0:T(8,128)S(1)}, f32[200,512]{1,0:T(8,128)S(1)}, u32[]{:S(2)}, u32[]{:S(2)}) collective-permute-start(f32[200,512]{1,0:T(8,128)S(1)} %add.155), channel_id=1, source_target_pairs={{0,4},{4,12},{12,20},{20,28},{28,24},{24,16},{16,8},{8,0},{9,17},{... | collective-permute-start | bytes 1228808 | tf_op jit(solution)/shard_map/ppermute | solution.py:286
  229.3 10.6 %collective-permute-start.47 = (f32[3,64,512]{2,1,0:T(8,128)S(1)}, f32[3,64,512]{2,1,0:T(8,128)S(1)}, u32[]{:S(2)}, u32[]{:S(2)}) collective-permute-start(f32[3,64,512]{2,1,0:T(8,128)S(1)} %collective-permute-done.46.refs_4_.turn_ref), channel_id=1, source_target_pairs={{0,4},{4,12},{12,20},{20,28},{28,24},{24,16},{16,8},{8,0},{9,17},{... | collective-permute-start | bytes 1179656 | tf_op jit(solution)/shard_map/ppermute | solution.py:286
  241.1 13.3 %collective-permute-start.54 = (f32[200,512]{1,0:T(8,128)S(1)}, f32[200,512]{1,0:T(8,128)S(1)}, u32[]{:S(2)}, u32[]{:S(2)}) collective-permute-start(f32[200,512]{1,0:T(8,128)S(1)} %add.156), channel_id=1, source_target_pairs={{0,4},{4,12},{12,20},{20,28},{28,24},{24,16},{16,8},{8,0},{9,17},{... | collective-permute-start | bytes 1228808 | tf_op jit(solution)/shard_map/ppermute | solution.py:286
  242.8 10.6 %collective-permute-start.48 = (f32[3,64,512]{2,1,0:T(8,128)S(1)}, f32[3,64,512]{2,1,0:T(8,128)S(1)}, u32[]{:S(2)}, u32[]{:S(2)}) collective-permute-start(f32[3,64,512]{2,1,0:T(8,128)S(1)} %collective-permute-done.47.refs_5_.turn_ref), channel_id=1, source_target_pairs={{0,4},{4,12},{12,20},{20,28},{28,24},{24,16},{16,8},{8,0},{9,17},{... | collective-permute-start | bytes 1179656 | tf_op jit(solution)/shard_map/ppermute | solution.py:286
  254.5 13.4 %collective-permute-start.55 = (f32[200,512]{1,0:T(8,128)S(1)}, f32[200,512]{1,0:T(8,128)S(1)}, u32[]{:S(2)}, u32[]{:S(2)}) collective-permute-start(f32[200,512]{1,0:T(8,128)S(1)} %add.157), channel_id=1, source_target_pairs={{0,4},{4,12},{12,20},{20,28},{28,24},{24,16},{16,8},{8,0},{9,17},{... | collective-permute-start | bytes 1228808 | tf_op jit(solution)/shard_map/ppermute | solution.py:286
  (73 other events, 832.8 us)

commit v2 on v1

v2 whole, which is shorter than its diff:
```python
from functools import partial

import jax
import jax.numpy as jnp
from jax import lax
from jax.experimental import pallas as pl
from jax.experimental.pallas import tpu as pltpu
from jax.sharding import PartitionSpec as P

EPSILON = 1e-06
VMEM_BYTES = 16 * 1024 * 1024
FIRST_VMEM, REST_VMEM = 60 * 1024 * 1024, 52 * 1024 * 1024
f32, bf16 = jnp.float32, jnp.bfloat16


def ring_order(count):
    width = max(w for w in range(1, count + 1) if count % w == 0 and w * w <= count)
    height = count // width
    if width == 1 or height % 2:
        return list(range(count))
    order = [0]
    for row in range(height):
        columns = range(1, width) if row % 2 == 0 else range(width - 1, 0, -1)
        order += [row * width + column for column in columns]
    return order + [row * width for row in range(height - 1, 0, -1)]


def ring_pairs(count, heads):
    order, pairs = ring_order(count), []
    for head in range(heads):
        way = order if head % 2 == 0 else order[::-1]
        pairs += [(way[at] * heads + head, way[(at + 1) % count] * heads + head) for at in range(count)]
    return pairs


def owner_at(order, step):
    device, sign = lax.axis_index("ctx"), 1 - 2 * lax.rem(lax.axis_index("head"), 2)
    count = len(order)
    at = sum(jnp.where(device == name, place, 0) for place, name in enumerate(order))
    place = lax.rem(at - sign * (1 + step) + 2 * count, count)
    return sum(jnp.where(place == i, name, 0) for i, name in enumerate(order))


def pair(x):
    high = x.astype(bf16)
    return high, (x - high.astype(f32)).astype(bf16)


def nt(a, b):
    return lax.dot_general(a, b, (((1,), (1,)), ((), ())), preferred_element_type=f32)


def nn(a, b):
    return lax.dot_general(a, b, (((1,), (0,)), ((), ())), preferred_element_type=f32)


def tn(a, b):
    return lax.dot_general(a, b, (((0,), (0,)), ((), ())), preferred_element_type=f32)


def three(dot, a, b):
    (a_high, a_low), (b_high, b_low) = a, b
    return dot(a_high, b_high) + (dot(a_high, b_low) + dot(a_low, b_high))


def rows_by(x, mats):
    pairs = [pair(m) for m in mats]
    stacked = jnp.concatenate([p[0] for p in pairs] + [p[1] for p in pairs], axis=0)
    both = nt(x, stacked)
    half = both.shape[1] // 2
    total = both[:, :half] + both[:, half:]
    rows = mats[0].shape[0]
    return [total[:, i * rows : (i + 1) * rows] for i in range(len(mats))]


def sums_by(parts, x):
    pairs = [pair(m) for m in parts]
    stacked = jnp.concatenate([p[0] for p in pairs] + [p[1] for p in pairs], axis=1)
    both = tn(stacked, x)
    half = both.shape[0] // 2
    total = both[:half] + both[half:]
    rows = parts[0].shape[1]
    return [total[i * rows : (i + 1) * rows] for i in range(len(parts))]


def silu_parts(gate):
    sig = 1.0 / (1.0 + jnp.exp(-gate))
    act = gate * sig
    return sig, act, sig + act * (1.0 - sig)


def to_columns(rows):
    count, tokens = rows.shape
    if count < 128:
        rows = jnp.concatenate([rows, jnp.zeros((128 - count, tokens), f32)], axis=0)
    turned = jnp.transpose(rows)
    return [turned[:, i : i + 1] for i in range(count)]


def to_rows(columns):
    tokens = columns[0].shape[0]
    lane = lax.broadcasted_iota(jnp.int32, (tokens, 128), 1)
    packed = jnp.zeros((tokens, 128), f32)
    for i, column in enumerate(columns):
        packed = jnp.where(lane == i, column, packed)
    return jnp.transpose(packed)[:8]


def minus_rate(rate_ref, factor):
    return -jnp.exp(to_columns(rate_ref[...])[0]) * factor


def write_parts(parts_ref, sums, steps):
    rows = sums[0].shape[0] // steps
    for step in range(steps):
        for i, total in enumerate(sums):
            parts_ref[3 * step + i][...] = total[step * rows : (step + 1) * rows]


def update_kernel(factor, order, first, steps, weights_ref, key_ref, value_ref, rate_ref, *refs):
    placed_ref, key_here, value_here, weight_sems, token_sems = refs[-5:]
    parts_ref, chunks_ref = refs[: 3 * steps], refs[3 * steps : -5]
    rows = weights_ref.shape[1] // len(order)
    copies = [pltpu.make_async_copy(key_ref, key_here, token_sems.at[0])]
    copies[0].start()
    for step in range(steps):
        source = weights_ref.at[:, pl.ds(pl.multiple_of(owner_at(order, first + step) * rows, rows), rows), :]
        copy = pltpu.make_async_copy(source, placed_ref.at[:, pl.ds(step * rows, rows), :], weight_sems.at[step])
        copy.start()
        copies.append(copy)
    copy = pltpu.make_async_copy(value_ref, value_here, token_sems.at[1])
    copy.start()
    rate = minus_rate(rate_ref, factor)
    for copy in copies + [copy]:
        copy.wait()
    keys, values = key_here[...], value_here[...]
    gate, up = rows_by(keys, [placed_ref[0], placed_ref[1]])
    (back,) = rows_by(values, [placed_ref[2]])
    _, act, slope = silu_parts(gate)
    back = back * rate
    grad_gate, grad_up = sums_by([back * up * slope, back * act], keys)
    (grad_down,) = sums_by([act * up * rate], values)
    write_parts(parts_ref, [grad_gate, grad_up, grad_down], steps)
    for step, chunk_ref in enumerate(chunks_ref):
        chunk_ref[...] = placed_ref[:, step * rows : (step + 1) * rows, :]


def scales(update, anchor):
    target = jnp.sqrt(jnp.sum(anchor * anchor, axis=-1, keepdims=True) + EPSILON)
    actual = jnp.sqrt(jnp.sum(update * update, axis=-1, keepdims=True) + EPSILON)
    return target, actual


def renorm_kernel(which, arrived_ref, mine_ref, anchor_ref, update_ref, new_ref):
    anchor = anchor_ref[which]
    update = anchor - (arrived_ref[...] + mine_ref[...])
    target, actual = scales(update, anchor)
    update_ref[...] = update
    new_ref[...] = update * (target / actual)


def renorm_back_kernel(anchor_ref, gain_one_ref, gain_two_ref, *refs):
    arrived, mine, updates, (turned_ref, direct_ref, gain_ref) = refs[:3], refs[3:6], refs[6:9], refs[9:]
    for i in range(3):
        anchor, update, cot = anchor_ref[i], updates[i][...], arrived[i][...] + mine[i][...]
        target, actual = scales(update, anchor)
        inner = jnp.sum(update * cot, axis=-1, keepdims=True)
        ratio = target / actual
        update_cot = ratio * cot - update * (inner * ratio / (actual * actual))
        turned_ref[i] = -update_cot
        direct_ref[i] = update_cot + anchor * (inner / (actual * target))
    gain_ref[...] = gain_one_ref[...] + gain_two_ref[...]


def forward_pass(queries, gate_mat, up_mat, down_mat):
    gate, up = rows_by(queries, [gate_mat, up_mat])
    _, act, _ = silu_parts(gate)
    out = three(nn, pair(act * up), pair(down_mat))
    return gate, up, out


def norm_sums(out, cotan, gain):
    return [jnp.sum(out * out, axis=1, keepdims=True), jnp.sum(gain * cotan * out, axis=1, keepdims=True)]


def forward_kernel(count, other, query_ref, cotan_ref, gain_ref, *refs):
    if other:
        other_ref, refs = refs[0], refs[1:]
    chunks, (weights_ref, gate_ref, up_ref, out_ref, stats_ref) = refs[:count], refs[count:]
    rows = weights_ref.shape[1] // (count if len(chunks[0].shape) == 3 else count // 3)
    for i, chunk in enumerate(chunks):
        if len(chunk.shape) == 3:
            weights_ref[:, i * rows : (i + 1) * rows, :] = chunk[...]
        else:
            weights_ref[i % 3, i // 3 * rows : (i // 3 + 1) * rows, :] = chunk[...]
    gate, up, out = forward_pass(query_ref[...], weights_ref[0], weights_ref[1], weights_ref[2])
    gate_ref[...] = gate
    up_ref[...] = up
    out_ref[...] = out
    sums = norm_sums(out, cotan_ref[...].astype(f32), gain_ref[...])
    if other:
        stats_ref[...] = to_rows([jnp.zeros((out.shape[0], 1), f32)] * 2 + sums) + other_ref[...]
    else:
        stats_ref[...] = to_rows(sums)


def backward_kernel(first, width, chunks, split, query_ref, cotan_ref, gain_ref, stats_ref, weights_ref, gate_ref, up_ref, out_ref, grad_gate_ref, grad_up_ref, gain_term_ref, *parts_ref):
    columns = to_columns(stats_ref[...])
    square, product = columns[first], columns[first + 1]
    inverse = 1.0 / jnp.sqrt(square / width + EPSILON)
    out, cotan = out_ref[...], cotan_ref[...].astype(f32)
    grad_out = gain_ref[...] * cotan * inverse - out * (inverse * inverse * inverse * product / width)
    gain_term_ref[...] = jnp.sum(cotan * out * inverse, axis=0, keepdims=True)
    up = up_ref[...]
    _, act, slope = silu_parts(gate_ref[...])
    grad_out = pair(grad_out)
    back = three(nt, grad_out, pair(weights_ref[2]))
    grad_gate, grad_up = back * up * slope, back * act
    grad_gate_ref[...] = grad_gate
    grad_up_ref[...] = grad_up
    sum_gate, sum_up = sums_by([grad_gate, grad_up], query_ref[...])
    sum_down = three(tn, pair(act * up), grad_out)
    if split:
        write_parts(parts_ref, [sum_gate, sum_up, sum_down], chunks)
    else:
        rows = sum_gate.shape[0] // chunks
        for step in range(chunks):
            for i, total in enumerate((sum_gate, sum_up, sum_down)):
                parts_ref[step][i] = total[step * rows : (step + 1) * rows]


def query_grad_kernel(grad_gate_ref, grad_up_ref, weights_ref, out_ref):
    total = three(nn, pair(grad_gate_ref[...]), pair(weights_ref[0]))
    total = total + three(nn, pair(grad_up_ref[...]), pair(weights_ref[1]))
    out_ref[...] = total.astype(bf16)


def second_order(keys, values, rate, weights, turns):
    gate, up, gate_turn, up_turn = rows_by(keys, [weights[0], weights[1], turns[0], turns[1]])
    back, back_turn = rows_by(values, [weights[2], turns[2]])
    back, back_turn = back * rate, back_turn * rate
    sig, act, slope = silu_parts(gate)
    bend = sig * (1.0 - sig) * (2.0 + gate * (1.0 - 2.0 * sig))
    hidden_turn = slope * gate_turn * up + act * up_turn
    cot_gate = back * (bend * gate_turn * up + slope * up_turn) + back_turn * up * slope
    cot_up = back * slope * gate_turn + back_turn * act
    return act * up, hidden_turn, cot_gate, cot_up, back * slope * up, back * act


def update_back_kernel(factor, order, step, first, last, key_ref, value_ref, rate_ref, weights_ref, turn_ref, gathered_ref, gain_ref, *refs):
    if first:
        direct_ref, refs = refs[0], refs[1:]
    else:
        before_key_ref, before_value_ref, refs = refs[0], refs[1], refs[2:]
    out_ref, grad_key_ref, grad_value_ref = refs[:3]
    keys, values = key_ref[...], value_ref[...]
    rate = minus_rate(rate_ref, factor)
    rows = weights_ref.shape[1]
    weights, turns = [weights_ref[i] for i in range(3)], [turn_ref[i] for i in range(3)]
    hidden, hidden_turn, cot_gate, cot_up, cot_gate_turn, cot_up_turn = second_order(keys, values, rate, weights, turns)
    sums = sums_by([cot_gate, cot_up], keys) + sums_by([hidden_turn * rate], values)
    for i, total in enumerate(sums):
        total = total + gathered_ref[i]
        out_ref[i * rows : (i + 1) * rows] = total + direct_ref[i] if first else total
    gain = jnp.broadcast_to(gain_ref[...], (8, gain_ref.shape[1]))
    piece = gain_ref.shape[1] // len(order)
    out_ref[3 * rows :] = pltpu.roll(gain, lax.rem((len(order) - owner_at(order, step)) * piece, gain_ref.shape[1]), 1)
    grad_key = three(nn, pair(jnp.concatenate([cot_gate, cot_up, cot_gate_turn, cot_up_turn], axis=1)), pair(jnp.concatenate([weights[0], weights[1], turns[0], turns[1]], axis=0)))
    grad_value = rate * three(nn, pair(jnp.concatenate([hidden_turn, hidden], axis=1)), pair(jnp.concatenate([weights[2], turns[2]], axis=0)))
    if not first:
        grad_key, grad_value = grad_key + before_key_ref[...], grad_value + before_value_ref[...]
    grad_key_ref[...] = grad_key.astype(grad_key_ref.dtype)
    grad_value_ref[...] = grad_value.astype(grad_value_ref.dtype)
    if last:
        refs[3][...] = to_rows([jnp.sum(grad_value * values.astype(f32), axis=1, keepdims=True)])[:1]


def finish_kernel(arrived_ref, mine_ref, weights_ref, gain_ref):
    rows = weights_ref.shape[1]
    for i in range(3):
        at = slice(i * rows, (i + 1) * rows)
        weights_ref[i] = arrived_ref[at] + mine_ref[at]
    gain_ref[...] = (arrived_ref[3 * rows :] + mine_ref[3 * rows :])[:1, : gain_ref.shape[1]]


def call(kernel, outs, *args, in_hbm=0, scratch=(), name=None, micros=4, vmem=VMEM_BYTES):
    in_specs = [pl.BlockSpec(memory_space=pl.ANY)] * in_hbm + [pl.BlockSpec(memory_space=pltpu.VMEM)] * (len(args) - in_hbm)
    return pl.pallas_call(
        kernel,
        out_shape=[jax.ShapeDtypeStruct(shape, dtype) for shape, dtype in outs],
        in_specs=in_specs,
        out_specs=[pl.BlockSpec(memory_space=pltpu.VMEM)] * len(outs),
        scratch_shapes=scratch,
        compiler_params=pltpu.CompilerParams(vmem_limit_bytes=vmem),
        cost_estimate=pl.CostEstimate(flops=int(micros * 1e9), transcendentals=0, bytes_accessed=int(micros * 3e6)),
        name=name,
    )(*args)


def local(chunks, heads, query_tokens, key_tokens, value_tokens, log_rate, fast_weights, norm_gain, out_grad):
    order, pairs = ring_order(chunks), ring_pairs(chunks, heads)

    def send(x):
        return lax.ppermute(x, ("ctx", "head"), pairs)

    weights = fast_weights[0]
    query_one, query_two = query_tokens[0, :, 0, :], query_tokens[1, :, 0, :]
    cotan_one, cotan_two = out_grad[0, :, 0, :], out_grad[1, :, 0, :]
    keys, values = key_tokens[:, 0, :], value_tokens[:, 0, :]
    tokens, width = keys.shape
    hidden = weights.shape[1]
    rows = hidden // chunks
    factor = (tokens * chunks * width) ** (-0.5)
    norm_width = heads * width
    token_f32, token_bf16, whole = ((tokens, width), f32), ((tokens, width), bf16), ((3, hidden, width), f32)
    hidden_f32, stats_shape, gain_shape = ((tokens, hidden), f32), ((8, tokens), f32), ((1, width), f32)
    chunk, part, packed = ((3, rows, width), f32), ((rows, width), f32), ((3 * rows + 8, width), f32)

    def scatter(parts):
        totals = list(parts[:3])
        for step in range(chunks - 1):
            totals = [send(t) for t in totals]
            if step < chunks - 2:
                totals = [t + p for t, p in zip(totals, parts[3 * step + 3 :])]
        return totals

    def update(first, steps, keep, vmem):
        return call(
            partial(update_kernel, factor, order, first, steps), [part] * (3 * steps) + ([chunk] * steps if keep else []), weights, keys, values, log_rate,
            in_hbm=3, vmem=vmem, name="update",
            scratch=[pltpu.VMEM((3, steps * rows, width), f32), pltpu.VMEM((tokens, width), bf16), pltpu.VMEM((tokens, width), bf16)]
            + [pltpu.SemaphoreType.DMA((steps,)), pltpu.SemaphoreType.DMA((2,))],
        )

    parts = update(0, 1, True, FIRST_VMEM)
    parts, placed = parts[:3], parts[3:]
    rest = update(1, chunks - 1, True, REST_VMEM)
    parts, placed = parts + rest[: -(chunks - 1)], placed + rest[-(chunks - 1) :]
    arrived = scatter(parts)
    old_weights, gate_one, up_one, out_one, stats_one = call(
        partial(forward_kernel, chunks, False), [whole, hidden_f32, hidden_f32, token_f32, stats_shape], query_one, cotan_one, norm_gain, *placed, name="forward_one"
    )
    updates, gathered = [], []
    for i in range(3):
        new = call(partial(renorm_kernel, i), [part] * 2, arrived[i], parts[i - 3], placed[-1], name="renorm")
        updates.append(new[0])
        gathered.append(new[1])
    held, gathered = gathered, []
    news = held
    for step in range(chunks - 1):
        held = [send(h) for h in held]
        gathered += held
    gathered += news

    new_weights, gate_two, up_two, out_two, stats = call(
        partial(forward_kernel, len(gathered), True), [whole, hidden_f32, hidden_f32, token_f32, stats_shape],
        query_two, cotan_two, norm_gain, stats_one, *gathered, name="forward_two",
    )
    if heads <= 4:
        others = [lax.ppermute(stats, "head", [(i, (i + d) % heads) for i in range(heads)]) for d in range(1, heads)]
        stats = sum(others, stats)
    else:
        stats = lax.psum(stats, "head")
    grad_gate, grad_up, gain_two, *parts = call(
        partial(backward_kernel, 2, norm_width, chunks, True), [hidden_f32, hidden_f32, gain_shape] + [part] * (3 * chunks),
        query_two, cotan_two, norm_gain, stats, new_weights, gate_two, up_two, out_two, name="backward_two",
    )
    arrived = scatter(parts)
    (grad_query_two,) = call(query_grad_kernel, [token_bf16], grad_gate, grad_up, new_weights, name="query_two")
    grad_gate, grad_up, gain_one, *direct_parts = call(
        partial(backward_kernel, 0, norm_width, chunks, False), [hidden_f32, hidden_f32, gain_shape] + [chunk] * chunks,
        query_one, cotan_one, norm_gain, stats, old_weights, gate_one, up_one, out_one, name="backward_one",
    )
    (grad_query_one,) = call(query_grad_kernel, [token_bf16], grad_gate, grad_up, old_weights, name="query_one")

    turn, direct, gain = call(
        renorm_back_kernel, [chunk, chunk, gain_shape], placed[-1], gain_one, gain_two, *arrived, *parts[-3:], *updates, name="renorm_back"
    )

    def back_at(step, turned, before, first=False, last=False):
        outs = [packed] + ([token_bf16, token_bf16, ((1, tokens), f32)] if last else [token_f32, token_f32])
        return call(
            partial(update_back_kernel, factor, order, step, first, last), outs, keys, values, log_rate, placed[step], turned, direct_parts[step], gain,
            *before, name="update_back",
        )

    own, *sums = back_at(chunks - 1, turn, [direct], first=True)
    total, held = None, turn
    for step in range(chunks - 1):
        held = send(held)
        mine_now, *sums = back_at(step, held, sums, last=step == chunks - 2)
        total = send(mine_now if total is None else total + mine_now)
    grad_key, grad_value, grad_rate = sums
    grad_weights, grad_gain = call(finish_kernel, [chunk, ((1, width // chunks), f32)], total, own, name="finish")
    grad_query = jnp.stack([grad_query_one, grad_query_two])[:, :, None, :]
    return grad_query, grad_key[:, None, :], grad_value[:, None, :], grad_rate, grad_weights[None], grad_gain


def solution(mesh):
    placed = (
        P(None, "ctx", "head", None),
        P("ctx", "head", None),
        P("ctx", "head", None),
        P("head", "ctx"),
        P("head", None, None, None),
        P("head", None),
        P(None, "ctx", "head", None),
    )
    return jax.shard_map(
        partial(local, mesh.shape["ctx"], mesh.shape["head"]),
        mesh=mesh,
        in_specs=placed,
        out_specs=(
            P(None, "ctx", "head", None),
            P("ctx", "head", None),
            P("ctx", "head", None),
            P("head", "ctx"),
            P("head", None, "ctx", None),
            P("head", "ctx"),
        ),
        check_vma=False,
    )
```

time: 270 us -> 204 us (0.76)
  waiting for transfers between devices: 98.9 us -> 64.5 us
  local copies, waits for them, and re-layouts: 25.3 us -> 0.15 us
  blocking collectives: 5.73 us -> 0 us
  starting transfers between devices: 96.8 us -> 102 us
  Pallas kernels: 37.8 us -> 33.5 us
    ppermute x56 -> x77, waiting for transfers between devices: 98.9 us -> 61.6 us  [send(): return lax.ppermute(x, ('ctx', 'head'), pairs)]
    unnamed x130 -> x40, local copies, waits for them, and re-layouts: 21.7 us -> 0.09 us
    psum x1 -> x0, blocking collectives: 5.73 us -> none  [local(): stats = lax.psum(stats, 'head')]
    pallas_call x19 -> x21, Pallas kernels: 37.8 us -> 33.5 us  [call(): pl.pallas_call(kernel, out_shape=[jax.ShapeDtypeStruct(shape, dtype) for...]
    ppermute x56 -> x77, starting transfers between devices: 96.8 us -> 100 us  [send(): return lax.ppermute(x, ('ctx', 'head'), pairs)]
    ppermute x0 -> x3, waiting for transfers between devices: none -> 2.91 us  [local(): lax.ppermute(stats, 'head', [(i, (i + d) % heads) for i in range(heads)])]
  transfers between devices with their start and end apart: 56 -> 80, of which waited for: 45 -> 62; matrix products, arithmetic and copies ran while one was open for 2% -> 1% of each run, Pallas kernels for 9% -> 12%
where the time goes in v2:
time: 204 us; the launch traced here: 203 us
  starting transfers between devices  102 us (50%)
  waiting for transfers between devices  64.5 us (32%)
  Pallas kernels  33.5 us (16%)
    ppermute x77, starting transfers between devices, send(): return lax.ppermute(x, ('ctx', 'head'), pairs)  100 us
    ppermute x77, waiting for transfers between devices, send(): return lax.ppermute(x, ('ctx', 'head'), pairs)  61.6 us
    pallas_call x21, Pallas kernels, call(): pl.pallas_call(kernel, out_shape=[jax.ShapeDtypeStruct(shape, dtype) for...  33.5 us
  transfers between devices with their start and end apart: 80, of which 62 were waited for; matrix products, arithmetic and copies ran while one was open for 1% of the time, Pallas kernels for 12%

profile of v2, /device:TPU:0, one launch (start us, length us, event | category | flops | bytes accessed | tf_op | source)
XLA Modules:
  0.0 203.4 jit_solution(8997116530448700360)
XLA Ops:
  0.6 3.4 %update.2 = (f32[64,512]{1,0:T(8,128)}, f32[64,512]{1,0:T(8,128)}, f32[64,512]{1,0:T(8,128)}, f32[3,64,512]{2,1,0:T(8,128)}) custom-call(f32[3,512,512]{2,1,0:T(8,128)} %bitcast.42, bf16[256,512]{1,0:T(8,128)(2,1)} %bitcast.22, bf16[256,512]{1,0:T(8,128)(2,1)} %bitcast.32, f32[1,256]{1,0:T(1,128)} %rate_ref.19), custom_call_target="tpu_custom_call" | custom-call | flops 4000000000 | bytes 12000000 | tf_op jit(solution)/shard_map/update/pallas_call | solution.py:288
  4.1 3.0 %collective-permute-start = (f32[64,512]{1,0:T(8,128)}, f32[64,512]{1,0:T(8,128)S(1)}, u32[]{:S(2)}, u32[]{:S(2)}) collective-permute-start(f32[64,512]{1,0:T(8,128)} %get-tuple-element.131), channel_id=1, source_target_pairs={{0,4},{4,12},{12,20},{20,28},{28,24},{24,16},{16,8},{8,0},{9,17},{... | collective-permute-start | bytes 393224 | tf_op jit(solution)/shard_map/ppermute | solution.py:304
  7.1 1.6 collective-permute-start.8
  8.7 1.6 collective-permute-start.16
  10.2 5.8 %update.3 = (f32[64,512]{1,0:T(8,128)S(1)}, f32[64,512]{1,0:T(8,128)S(1)}, f32[64,512]{1,0:T(8,128)S(1)}, f32[64,512]{1,0:T(8,128)S(1)}, f32[64,512]{1,0:T(8,128...) custom-call(f32[3,512,512]{2,1,0:T(8,128)} %bitcast.43, ...), custom_call_target="tpu_custom_call" | custom-call | flops 4000000000 | bytes 12000000 | tf_op jit(solution)/shard_map/update/pallas_call | solution.py:288
  16.1 1.6 collective-permute-start.1
  18.9 2.2 %collective-permute-done.1 = f32[64,512]{1,0:T(8,128)S(1)} collective-permute-done((f32[64,512]{1,0:T(8,128)S(1)}, f32[64,512]{1,0:T(8,128)S(1)}, u32[]{:S(2)}, u32[]{:S(2)}) %collective-permute-start.1) | collective-permute-done | bytes 131104 | tf_op jit(solution)/shard_map/ppermute | solution.py:304
  21.1 1.6 collective-permute-start.2
  26.2 1.6 collective-permute-start.3
  31.2 1.6 collective-permute-start.4
  36.3 1.6 collective-permute-start.5
  41.3 1.6 collective-permute-start.6
  46.5 1.6 collective-permute-start.7
  51.5 1.6 collective-permute-start.24
  56.5 1.6 collective-permute-start.27
  61.4 1.6 collective-permute-start.30
  66.4 1.6 collective-permute-start.33
  71.4 1.6 collective-permute-start.36
  76.3 1.6 collective-permute-start.39
  80.8 1.7 forward_one.1
  84.6 1.6 forward_two.1
  86.2 1.6 collective-permute-start.43
  88.0 2.0 collective-permute-done.43
  90.9 2.2 %backward_two.1 = (f32[256,512]{1,0:T(8,128)S(1)}, f32[256,512]{1,0:T(8,128)S(1)}, f32[1,512]{1,0:T(1,128)S(1)}, f32[64,512]{1,0:T(8,128)S(1)}, f32[64,512]{1,0:...) custom-call(bf16[256,512]{1,0:T(8,128)(2,1)S(1)} %get-tuple-element., ...), custom_call_target="tpu_custom_call" | custom-call | flops 4000000000 | bytes 12000000 | tf_op jit(solution)/shard_map/backward_two/pallas_call | solution.py:288
  95.4 2.8 %collective-permute-done.45 = f32[64,512]{1,0:T(8,128)S(1)} collective-permute-done((f32[64,512]{1,0:T(8,128)S(1)}, f32[64,512]{1,0:T(8,128)S(1)}, u32[]{:S(2)}, u32[]{:S(2)}) %collective-permute-start.45) | collective-permute-done | bytes 131104 | tf_op jit(solution)/shard_map/ppermute | solution.py:304
  127.5 2.3 %backward_one.1 = (f32[256,512]{1,0:T(8,128)S(1)}, f32[256,512]{1,0:T(8,128)S(1)}, f32[1,512]{1,0:T(1,128)S(1)}, f32[3,64,512]{2,1,0:T(8,128)S(1)}, f32[3,64,512...) custom-call(bf16[256,512]{1,0:T(8,128)(2,1)S(1)} %get-tuple-element., ...), custom_call_target="tpu_custom_call" | custom-call | flops 4000000000 | bytes 12000000 | tf_op jit(solution)/shard_map/backward_one/pallas_call | solution.py:288
  132.8 1.5 update_back.8
  134.4 5.0 %collective-permute-done.66.turn_ref = f32[3,64,512]{2,1,0:T(8,128)S(1)} collective-permute-done((f32[3,64,512]{2,1,0:T(8,128)S(1)}, f32[3,64,512]{2,1,0:T(8,128)S(1)}, u32[]{:S(2)}, u32[]{:S(2)}) %collective-permute-start.66) | collective-permute-done | bytes 393248 | tf_op jit(solution)/shard_map/ppermute | solution.py:304
  140.6 1.5 update_back.9
  142.7 4.5 %collective-permute-done.67.turn_ref = f32[3,64,512]{2,1,0:T(8,128)S(1)} collective-permute-done((f32[3,64,512]{2,1,0:T(8,128)S(1)}, f32[3,64,512]{2,1,0:T(8,128)S(1)}, u32[]{:S(2)}, u32[]{:S(2)}) %collective-permute-start.67) | collective-permute-done | bytes 393248 | tf_op jit(solution)/shard_map/ppermute | solution.py:304
  148.4 1.5 update_back.10
  149.9 1.7 collective-permute-done.73
  152.9 2.9 %collective-permute-done.68.turn_ref = f32[3,64,512]{2,1,0:T(8,128)S(1)} collective-permute-done((f32[3,64,512]{2,1,0:T(8,128)S(1)}, f32[3,64,512]{2,1,0:T(8,128)S(1)}, u32[]{:S(2)}, u32[]{:S(2)}) %collective-permute-start.68) | collective-permute-done | bytes 393248 | tf_op jit(solution)/shard_map/ppermute | solution.py:304
  157.0 1.5 update_back.11
  158.5 1.7 collective-permute-done.74
  161.5 2.9 %collective-permute-done.69.turn_ref = f32[3,64,512]{2,1,0:T(8,128)S(1)} collective-permute-done((f32[3,64,512]{2,1,0:T(8,128)S(1)}, f32[3,64,512]{2,1,0:T(8,128)S(1)}, u32[]{:S(2)}, u32[]{:S(2)}) %collective-permute-start.69) | collective-permute-done | bytes 393248 | tf_op jit(solution)/shard_map/ppermute | solution.py:304
  165.6 1.5 update_back.12
  167.1 1.7 collective-permute-done.75
  170.1 2.9 %collective-permute-done.70.turn_ref = f32[3,64,512]{2,1,0:T(8,128)S(1)} collective-permute-done((f32[3,64,512]{2,1,0:T(8,128)S(1)}, f32[3,64,512]{2,1,0:T(8,128)S(1)}, u32[]{:S(2)}, u32[]{:S(2)}) %collective-permute-start.70) | collective-permute-done | bytes 393248 | tf_op jit(solution)/shard_map/ppermute | solution.py:304
  174.2 1.5 update_back.13
  175.7 1.7 collective-permute-done.76
  178.7 2.9 %collective-permute-done.71.turn_ref = f32[3,64,512]{2,1,0:T(8,128)S(1)} collective-permute-done((f32[3,64,512]{2,1,0:T(8,128)S(1)}, f32[3,64,512]{2,1,0:T(8,128)S(1)}, u32[]{:S(2)}, u32[]{:S(2)}) %collective-permute-start.71) | collective-permute-done | bytes 393248 | tf_op jit(solution)/shard_map/ppermute | solution.py:304
  182.8 1.5 update_back.14
  184.3 1.7 collective-permute-done.77
  188.4 1.8 collective-permute-done.72.turn_ref
  190.2 2.3 %update_back.15 = (f32[200,512]{1,0:T(8,128)S(1)}, bf16[256,512]{1,0:T(8,128)(2,1)}, bf16[256,512]{1,0:T(8,128)(2,1)}, f32[1,256]{1,0:T(1,128)}) custom-call(bf16[256,512]{1,0:T(8,128)(2,1)S(1)} %bitcast.31, bf16[256,512]{1,0:T(8,128)(2,1)S(1)} %bitcast.41, f32[1,256]{1,0:T(1,128)S(1)} %copy-done.3, f32[3,64,512]{2,1,0:T(8,128)S(1)} %copy-done.4, ...), custom_call_target="tpu_custom_call" | custom-call | flops 4000000000 | bytes 12000000 | tf_op jit(solution)/shard_map/update_back/pallas_call | solution.py:288
  192.5 2.1 %collective-permute-done.78 = f32[200,512]{1,0:T(8,128)S(1)} collective-permute-done((f32[200,512]{1,0:T(8,128)S(1)}, f32[200,512]{1,0:T(8,128)S(1)}, u32[]{:S(2)}, u32[]{:S(2)}) %collective-permute-start.78) | collective-permute-done | bytes 409632 | tf_op jit(solution)/shard_map/ppermute | solution.py:304
  197.8 4.8 %collective-permute-done.79.arrived_ref = f32[200,512]{1,0:T(8,128)S(1)} collective-permute-done((f32[200,512]{1,0:T(8,128)S(1)}, f32[200,512]{1,0:T(8,128)S(1)}, u32[]{:S(2)}, u32[]{:S(2)}) %collective-permute-start.79) | collective-permute-done | bytes 409632 | tf_op jit(solution)/shard_map/ppermute | solution.py:304
  (218 shorter events, 98.8 us)
Async XLA Ops:
  4.1 12.0 %collective-permute-start = (f32[64,512]{1,0:T(8,128)}, f32[64,512]{1,0:T(8,128)S(1)}, u32[]{:S(2)}, u32[]{:S(2)}) collective-permute-start(f32[64,512]{1,0:T(8,128)} %get-tuple-element.131), channel_id=1, source_target_pairs={{0,4},{4,12},{12,20},{20,28},{28,24},{24,16},{16,8},{8,0},{9,17},{... | collective-permute-start | bytes 393224 | tf_op jit(solution)/shard_map/ppermute | solution.py:304
  7.1 10.6 %collective-permute-start.8 = (f32[64,512]{1,0:T(8,128)}, f32[64,512]{1,0:T(8,128)S(1)}, u32[]{:S(2)}, u32[]{:S(2)}) collective-permute-start(f32[64,512]{1,0:T(8,128)} %get-tuple-element.140), channel_id=1, source_target_pairs={{0,4},{4,12},{12,20},{20,28},{28,24},{24,16},{16,8},{8,0},{9,17},{... | collective-permute-start | bytes 393224 | tf_op jit(solution)/shard_map/ppermute | solution.py:304
  8.7 9.7 %collective-permute-start.16 = (f32[64,512]{1,0:T(8,128)}, f32[64,512]{1,0:T(8,128)S(1)}, u32[]{:S(2)}, u32[]{:S(2)}) collective-permute-start(f32[64,512]{1,0:T(8,128)} %get-tuple-element.149), channel_id=1, source_target_pairs={{0,4},{4,12},{12,20},{20,28},{28,24},{24,16},{16,8},{8,0},{9,17},{... | collective-permute-start | bytes 393224 | tf_op jit(solution)/shard_map/ppermute | solution.py:304
  16.1 5.0 %collective-permute-start.1 = (f32[64,512]{1,0:T(8,128)S(1)}, f32[64,512]{1,0:T(8,128)S(1)}, u32[]{:S(2)}, u32[]{:S(2)}) collective-permute-start(f32[64,512]{1,0:T(8,128)S(1)} %add.135), channel_id=1, source_target_pairs={{0,4},{4,12},{12,20},{20,28},{28,24},{24,16},{16,8},{8,0},{9,17},{... | collective-permute-start | bytes 393224 | tf_op jit(solution)/shard_map/ppermute | solution.py:304
  17.7 5.0 %collective-permute-start.9 = (f32[64,512]{1,0:T(8,128)S(1)}, f32[64,512]{1,0:T(8,128)S(1)}, u32[]{:S(2)}, u32[]{:S(2)}) collective-permute-start(f32[64,512]{1,0:T(8,128)S(1)} %add.141), channel_id=1, source_target_pairs={{0,4},{4,12},{12,20},{20,28},{28,24},{24,16},{16,8},{8,0},{9,17},{... | collective-permute-start | bytes 393224 | tf_op jit(solution)/shard_map/ppermute | solution.py:304
  18.4 5.8 %collective-permute-start.17 = (f32[64,512]{1,0:T(8,128)S(1)}, f32[64,512]{1,0:T(8,128)S(1)}, u32[]{:S(2)}, u32[]{:S(2)}) collective-permute-start(f32[64,512]{1,0:T(8,128)S(1)} %add.147), channel_id=1, source_target_pairs={{0,4},{4,12},{12,20},{20,28},{28,24},{24,16},{16,8},{8,0},{9,17},{... | collective-permute-start | bytes 393224 | tf_op jit(solution)/shard_map/ppermute | solution.py:304
  21.1 5.0 %collective-permute-start.2 = (f32[64,512]{1,0:T(8,128)S(1)}, f32[64,512]{1,0:T(8,128)S(1)}, u32[]{:S(2)}, u32[]{:S(2)}) collective-permute-start(f32[64,512]{1,0:T(8,128)S(1)} %add.136), channel_id=1, source_target_pairs={{0,4},{4,12},{12,20},{20,28},{28,24},{24,16},{16,8},{8,0},{9,17},{... | collective-permute-start | bytes 393224 | tf_op jit(solution)/shard_map/ppermute | solution.py:304
  22.8 5.0 %collective-permute-start.10 = (f32[64,512]{1,0:T(8,128)S(1)}, f32[64,512]{1,0:T(8,128)S(1)}, u32[]{:S(2)}, u32[]{:S(2)}) collective-permute-start(f32[64,512]{1,0:T(8,128)S(1)} %add.142), channel_id=1, source_target_pairs={{0,4},{4,12},{12,20},{20,28},{28,24},{24,16},{16,8},{8,0},{9,17},{... | collective-permute-start | bytes 393224 | tf_op jit(solution)/shard_map/ppermute | solution.py:304
  24.2 5.0 %collective-permute-start.18 = (f32[64,512]{1,0:T(8,128)S(1)}, f32[64,512]{1,0:T(8,128)S(1)}, u32[]{:S(2)}, u32[]{:S(2)}) collective-permute-start(f32[64,512]{1,0:T(8,128)S(1)} %add.148), channel_id=1, source_target_pairs={{0,4},{4,12},{12,20},{20,28},{28,24},{24,16},{16,8},{8,0},{9,17},{... | collective-permute-start | bytes 393224 | tf_op jit(solution)/shard_map/ppermute | solution.py:304
  26.2 5.0 %collective-permute-start.3 = (f32[64,512]{1,0:T(8,128)S(1)}, f32[64,512]{1,0:T(8,128)S(1)}, u32[]{:S(2)}, u32[]{:S(2)}) collective-permute-start(f32[64,512]{1,0:T(8,128)S(1)} %add.137), channel_id=1, source_target_pairs={{0,4},{4,12},{12,20},{20,28},{28,24},{24,16},{16,8},{8,0},{9,17},{... | collective-permute-start | bytes 393224 | tf_op jit(solution)/shard_map/ppermute | solution.py:304
  27.8 5.0 %collective-permute-start.11 = (f32[64,512]{1,0:T(8,128)S(1)}, f32[64,512]{1,0:T(8,128)S(1)}, u32[]{:S(2)}, u32[]{:S(2)}) collective-permute-start(f32[64,512]{1,0:T(8,128)S(1)} %add.143), channel_id=1, source_target_pairs={{0,4},{4,12},{12,20},{20,28},{28,24},{24,16},{16,8},{8,0},{9,17},{... | collective-permute-start | bytes 393224 | tf_op jit(solution)/shard_map/ppermute | solution.py:304
  29.2 5.0 %collective-permute-start.19 = (f32[64,512]{1,0:T(8,128)S(1)}, f32[64,512]{1,0:T(8,128)S(1)}, u32[]{:S(2)}, u32[]{:S(2)}) collective-permute-start(f32[64,512]{1,0:T(8,128)S(1)} %add.149), channel_id=1, source_target_pairs={{0,4},{4,12},{12,20},{20,28},{28,24},{24,16},{16,8},{8,0},{9,17},{... | collective-permute-start | bytes 393224 | tf_op jit(solution)/shard_map/ppermute | solution.py:304
  31.2 5.0 %collective-permute-start.4 = (f32[64,512]{1,0:T(8,128)S(1)}, f32[64,512]{1,0:T(8,128)S(1)}, u32[]{:S(2)}, u32[]{:S(2)}) collective-permute-start(f32[64,512]{1,0:T(8,128)S(1)} %add.138), channel_id=1, source_target_pairs={{0,4},{4,12},{12,20},{20,28},{28,24},{24,16},{16,8},{8,0},{9,17},{... | collective-permute-start | bytes 393224 | tf_op jit(solution)/shard_map/ppermute | solution.py:304
  32.9 5.0 %collective-permute-start.12 = (f32[64,512]{1,0:T(8,128)S(1)}, f32[64,512]{1,0:T(8,128)S(1)}, u32[]{:S(2)}, u32[]{:S(2)}) collective-permute-start(f32[64,512]{1,0:T(8,128)S(1)} %add.144), channel_id=1, source_target_pairs={{0,4},{4,12},{12,20},{20,28},{28,24},{24,16},{16,8},{8,0},{9,17},{... | collective-permute-start | bytes 393224 | tf_op jit(solution)/shard_map/ppermute | solution.py:304
  34.3 5.0 %collective-permute-start.20 = (f32[64,512]{1,0:T(8,128)S(1)}, f32[64,512]{1,0:T(8,128)S(1)}, u32[]{:S(2)}, u32[]{:S(2)}) collective-permute-start(f32[64,512]{1,0:T(8,128)S(1)} %add.150), channel_id=1, source_target_pairs={{0,4},{4,12},{12,20},{20,28},{28,24},{24,16},{16,8},{8,0},{9,17},{... | collective-permute-start | bytes 393224 | tf_op jit(solution)/shard_map/ppermute | solution.py:304
  36.3 5.0 %collective-permute-start.5 = (f32[64,512]{1,0:T(8,128)S(1)}, f32[64,512]{1,0:T(8,128)S(1)}, u32[]{:S(2)}, u32[]{:S(2)}) collective-permute-start(f32[64,512]{1,0:T(8,128)S(1)} %add.139), channel_id=1, source_target_pairs={{0,4},{4,12},{12,20},{20,28},{28,24},{24,16},{16,8},{8,0},{9,17},{... | collective-permute-start | bytes 393224 | tf_op jit(solution)/shard_map/ppermute | solution.py:304
  37.9 5.0 %collective-permute-start.13 = (f32[64,512]{1,0:T(8,128)S(1)}, f32[64,512]{1,0:T(8,128)S(1)}, u32[]{:S(2)}, u32[]{:S(2)}) collective-permute-start(f32[64,512]{1,0:T(8,128)S(1)} %add.145), channel_id=1, source_target_pairs={{0,4},{4,12},{12,20},{20,28},{28,24},{24,16},{16,8},{8,0},{9,17},{... | collective-permute-start | bytes 393224 | tf_op jit(solution)/shard_map/ppermute | solution.py:304
  39.3 5.0 %collective-permute-start.21 = (f32[64,512]{1,0:T(8,128)S(1)}, f32[64,512]{1,0:T(8,128)S(1)}, u32[]{:S(2)}, u32[]{:S(2)}) collective-permute-start(f32[64,512]{1,0:T(8,128)S(1)} %add.151), channel_id=1, source_target_pairs={{0,4},{4,12},{12,20},{20,28},{28,24},{24,16},{16,8},{8,0},{9,17},{... | collective-permute-start | bytes 393224 | tf_op jit(solution)/shard_map/ppermute | solution.py:304
  41.3 5.0 %collective-permute-start.6 = (f32[64,512]{1,0:T(8,128)S(1)}, f32[64,512]{1,0:T(8,128)S(1)}, u32[]{:S(2)}, u32[]{:S(2)}) collective-permute-start(f32[64,512]{1,0:T(8,128)S(1)} %add.140), channel_id=1, source_target_pairs={{0,4},{4,12},{12,20},{20,28},{28,24},{24,16},{16,8},{8,0},{9,17},{... | collective-permute-start | bytes 393224 | tf_op jit(solution)/shard_map/ppermute | solution.py:304
  43.0 5.1 %collective-permute-start.14 = (f32[64,512]{1,0:T(8,128)S(1)}, f32[64,512]{1,0:T(8,128)S(1)}, u32[]{:S(2)}, u32[]{:S(2)}) collective-permute-start(f32[64,512]{1,0:T(8,128)S(1)} %add.146), channel_id=1, source_target_pairs={{0,4},{4,12},{12,20},{20,28},{28,24},{24,16},{16,8},{8,0},{9,17},{... | collective-permute-start | bytes 393224 | tf_op jit(solution)/shard_map/ppermute | solution.py:304
  44.4 5.1 %collective-permute-start.22 = (f32[64,512]{1,0:T(8,128)S(1)}, f32[64,512]{1,0:T(8,128)S(1)}, u32[]{:S(2)}, u32[]{:S(2)}) collective-permute-start(f32[64,512]{1,0:T(8,128)S(1)} %add.152), channel_id=1, source_target_pairs={{0,4},{4,12},{12,20},{20,28},{28,24},{24,16},{16,8},{8,0},{9,17},{... | collective-permute-start | bytes 393224 | tf_op jit(solution)/shard_map/ppermute | solution.py:304
  46.5 5.0 %collective-permute-start.7 = (f32[64,512]{1,0:T(8,128)S(1)}, f32[64,512]{1,0:T(8,128)S(1)}, u32[]{:S(2)}, u32[]{:S(2)}) collective-permute-start(f32[64,512]{1,0:T(8,128)S(1)} %get-tuple-element.139.refs_22_), channel_id=1, source_target_pairs={{0,4},{4,12},{12,20},{20,28},{28,24},{24,16},{16,8},{8,0},{9,17},{... | collective-permute-start | bytes 393224 | tf_op jit(solution)/shard_map/ppermute | solution.py:304
  48.2 5.0 %collective-permute-start.15 = (f32[64,512]{1,0:T(8,128)S(1)}, f32[64,512]{1,0:T(8,128)S(1)}, u32[]{:S(2)}, u32[]{:S(2)}) collective-permute-start(f32[64,512]{1,0:T(8,128)S(1)} %get-tuple-element.148.refs_23_), channel_id=1, source_target_pairs={{0,4},{4,12},{12,20},{20,28},{28,24},{24,16},{16,8},{8,0},{9,17},{... | collective-permute-start | bytes 393224 | tf_op jit(solution)/shard_map/ppermute | solution.py:304
  49.7 5.0 %collective-permute-start.23 = (f32[64,512]{1,0:T(8,128)S(1)}, f32[64,512]{1,0:T(8,128)S(1)}, u32[]{:S(2)}, u32[]{:S(2)}) collective-permute-start(f32[64,512]{1,0:T(8,128)S(1)} %get-tuple-element.157.refs_24_), channel_id=1, source_target_pairs={{0,4},{4,12},{12,20},{20,28},{28,24},{24,16},{16,8},{8,0},{9,17},{... | collective-permute-start | bytes 393224 | tf_op jit(solution)/shard_map/ppermute | solution.py:304
  76.3 6.2 %collective-permute-start.39 = (f32[64,512]{1,0:T(8,128)S(1)}, f32[64,512]{1,0:T(8,128)S(1)}, u32[]{:S(2)}, u32[]{:S(2)}) collective-permute-start(f32[64,512]{1,0:T(8,128)S(1)} %collective-permute-done.36.refs_16_), channel_id=1, source_target_pairs={{0,4},{4,12},{12,20},{20,28},{28,24},{24,16},{16,8},{8,0},{9,17},{... | collective-permute-start | bytes 393224 | tf_op jit(solution)/shard_map/ppermute | solution.py:304
  93.1 5.0 %collective-permute-start.45 = (f32[64,512]{1,0:T(8,128)S(1)}, f32[64,512]{1,0:T(8,128)S(1)}, u32[]{:S(2)}, u32[]{:S(2)}) collective-permute-start(f32[64,512]{1,0:T(8,128)S(1)} %get-tuple-element.173), channel_id=1, source_target_pairs={{0,4},{4,12},{12,20},{20,28},{28,24},{24,16},{16,8},{8,0},{9,17},{... | collective-permute-start | bytes 393224 | tf_op jit(solution)/shard_map/ppermute | solution.py:304
  94.4 5.2 %collective-permute-start.52 = (f32[64,512]{1,0:T(8,128)S(1)}, f32[64,512]{1,0:T(8,128)S(1)}, u32[]{:S(2)}, u32[]{:S(2)}) collective-permute-start(f32[64,512]{1,0:T(8,128)S(1)} %get-tuple-element.180), channel_id=1, source_target_pairs={{0,4},{4,12},{12,20},{20,28},{28,24},{24,16},{16,8},{8,0},{9,17},{... | collective-permute-start | bytes 393224 | tf_op jit(solution)/shard_map/ppermute | solution.py:304
  94.9 6.0 %collective-permute-start.59 = (f32[64,512]{1,0:T(8,128)S(1)}, f32[64,512]{1,0:T(8,128)S(1)}, u32[]{:S(2)}, u32[]{:S(2)}) collective-permute-start(f32[64,512]{1,0:T(8,128)S(1)} %get-tuple-element.187), channel_id=1, source_target_pairs={{0,4},{4,12},{12,20},{20,28},{28,24},{24,16},{16,8},{8,0},{9,17},{... | collective-permute-start | bytes 393224 | tf_op jit(solution)/shard_map/ppermute | solution.py:304
  98.2 5.0 %collective-permute-start.46 = (f32[64,512]{1,0:T(8,128)S(1)}, f32[64,512]{1,0:T(8,128)S(1)}, u32[]{:S(2)}, u32[]{:S(2)}) collective-permute-start(f32[64,512]{1,0:T(8,128)S(1)} %add.156), channel_id=1, source_target_pairs={{0,4},{4,12},{12,20},{20,28},{28,24},{24,16},{16,8},{8,0},{9,17},{... | collective-permute-start | bytes 393224 | tf_op jit(solution)/shard_map/ppermute | solution.py:304
  99.6 5.0 %collective-permute-start.53 = (f32[64,512]{1,0:T(8,128)S(1)}, f32[64,512]{1,0:T(8,128)S(1)}, u32[]{:S(2)}, u32[]{:S(2)}) collective-permute-start(f32[64,512]{1,0:T(8,128)S(1)} %add.162), channel_id=1, source_target_pairs={{0,4},{4,12},{12,20},{20,28},{28,24},{24,16},{16,8},{8,0},{9,17},{... | collective-permute-start | bytes 393224 | tf_op jit(solution)/shard_map/ppermute | solution.py:304
  101.0 5.0 %collective-permute-start.60 = (f32[64,512]{1,0:T(8,128)S(1)}, f32[64,512]{1,0:T(8,128)S(1)}, u32[]{:S(2)}, u32[]{:S(2)}) collective-permute-start(f32[64,512]{1,0:T(8,128)S(1)} %add.168), channel_id=1, source_target_pairs={{0,4},{4,12},{12,20},{20,28},{28,24},{24,16},{16,8},{8,0},{9,17},{... | collective-permute-start | bytes 393224 | tf_op jit(solution)/shard_map/ppermute | solution.py:304
  103.2 5.0 %collective-permute-start.47 = (f32[64,512]{1,0:T(8,128)S(1)}, f32[64,512]{1,0:T(8,128)S(1)}, u32[]{:S(2)}, u32[]{:S(2)}) collective-permute-start(f32[64,512]{1,0:T(8,128)S(1)} %add.157), channel_id=1, source_target_pairs={{0,4},{4,12},{12,20},{20,28},{28,24},{24,16},{16,8},{8,0},{9,17},{... | collective-permute-start | bytes 393224 | tf_op jit(solution)/shard_map/ppermute | solution.py:304
  104.6 5.0 %collective-permute-start.54 = (f32[64,512]{1,0:T(8,128)S(1)}, f32[64,512]{1,0:T(8,128)S(1)}, u32[]{:S(2)}, u32[]{:S(2)}) collective-permute-start(f32[64,512]{1,0:T(8,128)S(1)} %add.163), channel_id=1, source_target_pairs={{0,4},{4,12},{12,20},{20,28},{28,24},{24,16},{16,8},{8,0},{9,17},{... | collective-permute-start | bytes 393224 | tf_op jit(solution)/shard_map/ppermute | solution.py:304
  123.4 6.3 %collective-permute-start.51 = (f32[64,512]{1,0:T(8,128)S(1)}, f32[64,512]{1,0:T(8,128)S(1)}, u32[]{:S(2)}, u32[]{:S(2)}) collective-permute-start(f32[64,512]{1,0:T(8,128)S(1)} %add.161), channel_id=1, source_target_pairs={{0,4},{4,12},{12,20},{20,28},{28,24},{24,16},{16,8},{8,0},{9,17},{... | collective-permute-start | bytes 393224 | tf_op jit(solution)/shard_map/ppermute | solution.py:304
  131.6 7.8 %collective-permute-start.66 = (f32[3,64,512]{2,1,0:T(8,128)S(1)}, f32[3,64,512]{2,1,0:T(8,128)S(1)}, u32[]{:S(2)}, u32[]{:S(2)}) collective-permute-start(f32[3,64,512]{2,1,0:T(8,128)S(1)} %get-tuple-element.200.turn_ref), channel_id=1, source_target_pairs={{0,4},{4,12},{12,20},{20,28},{28,24},{24,16},{16,8},{8,0},{9,17},{... | collective-permute-start | bytes 1179656 | tf_op jit(solution)/shard_map/ppermute | solution.py:304
  139.4 7.8 %collective-permute-start.67 = (f32[3,64,512]{2,1,0:T(8,128)S(1)}, f32[3,64,512]{2,1,0:T(8,128)S(1)}, u32[]{:S(2)}, u32[]{:S(2)}) collective-permute-start(f32[3,64,512]{2,1,0:T(8,128)S(1)} %collective-permute-done.66.turn_ref), channel_id=1, source_target_pairs={{0,4},{4,12},{12,20},{20,28},{28,24},{24,16},{16,8},{8,0},{9,17},{... | collective-permute-start | bytes 1179656 | tf_op jit(solution)/shard_map/ppermute | solution.py:304
  142.1 9.4 %collective-permute-start.73 = (f32[200,512]{1,0:T(8,128)S(1)}, f32[200,512]{1,0:T(8,128)S(1)}, u32[]{:S(2)}, u32[]{:S(2)}) collective-permute-start(f32[200,512]{1,0:T(8,128)S(1)} %get-tuple-element.228), channel_id=1, source_target_pairs={{0,4},{4,12},{12,20},{20,28},{28,24},{24,16},{16,8},{8,0},{9,17},{... | collective-permute-start | bytes 1228808 | tf_op jit(solution)/shard_map/ppermute | solution.py:304
  147.2 8.6 %collective-permute-start.68 = (f32[3,64,512]{2,1,0:T(8,128)S(1)}, f32[3,64,512]{2,1,0:T(8,128)S(1)}, u32[]{:S(2)}, u32[]{:S(2)}) collective-permute-start(f32[3,64,512]{2,1,0:T(8,128)S(1)} %collective-permute-done.67.turn_ref), channel_id=1, source_target_pairs={{0,4},{4,12},{12,20},{20,28},{28,24},{24,16},{16,8},{8,0},{9,17},{... | collective-permute-start | bytes 1179656 | tf_op jit(solution)/shard_map/ppermute | solution.py:304
  151.6 8.5 %collective-permute-start.74 = (f32[200,512]{1,0:T(8,128)S(1)}, f32[200,512]{1,0:T(8,128)S(1)}, u32[]{:S(2)}, u32[]{:S(2)}) collective-permute-start(f32[200,512]{1,0:T(8,128)S(1)} %add.174), channel_id=1, source_target_pairs={{0,4},{4,12},{12,20},{20,28},{28,24},{24,16},{16,8},{8,0},{9,17},{... | collective-permute-start | bytes 1228808 | tf_op jit(solution)/shard_map/ppermute | solution.py:304
  155.8 8.6 %collective-permute-start.69 = (f32[3,64,512]{2,1,0:T(8,128)S(1)}, f32[3,64,512]{2,1,0:T(8,128)S(1)}, u32[]{:S(2)}, u32[]{:S(2)}) collective-permute-start(f32[3,64,512]{2,1,0:T(8,128)S(1)} %collective-permute-done.68.turn_ref), channel_id=1, source_target_pairs={{0,4},{4,12},{12,20},{20,28},{28,24},{24,16},{16,8},{8,0},{9,17},{... | collective-permute-start | bytes 1179656 | tf_op jit(solution)/shard_map/ppermute | solution.py:304
  160.2 8.5 %collective-permute-start.75 = (f32[200,512]{1,0:T(8,128)S(1)}, f32[200,512]{1,0:T(8,128)S(1)}, u32[]{:S(2)}, u32[]{:S(2)}) collective-permute-start(f32[200,512]{1,0:T(8,128)S(1)} %add.175), channel_id=1, source_target_pairs={{0,4},{4,12},{12,20},{20,28},{28,24},{24,16},{16,8},{8,0},{9,17},{... | collective-permute-start | bytes 1228808 | tf_op jit(solution)/shard_map/ppermute | solution.py:304
  164.4 8.6 %collective-permute-start.70 = (f32[3,64,512]{2,1,0:T(8,128)S(1)}, f32[3,64,512]{2,1,0:T(8,128)S(1)}, u32[]{:S(2)}, u32[]{:S(2)}) collective-permute-start(f32[3,64,512]{2,1,0:T(8,128)S(1)} %collective-permute-done.69.turn_ref), channel_id=1, source_target_pairs={{0,4},{4,12},{12,20},{20,28},{28,24},{24,16},{16,8},{8,0},{9,17},{... | collective-permute-start | bytes 1179656 | tf_op jit(solution)/shard_map/ppermute | solution.py:304
  168.8 8.5 %collective-permute-start.76 = (f32[200,512]{1,0:T(8,128)S(1)}, f32[200,512]{1,0:T(8,128)S(1)}, u32[]{:S(2)}, u32[]{:S(2)}) collective-permute-start(f32[200,512]{1,0:T(8,128)S(1)} %add.176), channel_id=1, source_target_pairs={{0,4},{4,12},{12,20},{20,28},{28,24},{24,16},{16,8},{8,0},{9,17},{... | collective-permute-start | bytes 1228808 | tf_op jit(solution)/shard_map/ppermute | solution.py:304
  173.0 8.6 %collective-permute-start.71 = (f32[3,64,512]{2,1,0:T(8,128)S(1)}, f32[3,64,512]{2,1,0:T(8,128)S(1)}, u32[]{:S(2)}, u32[]{:S(2)}) collective-permute-start(f32[3,64,512]{2,1,0:T(8,128)S(1)} %collective-permute-done.70.turn_ref), channel_id=1, source_target_pairs={{0,4},{4,12},{12,20},{20,28},{28,24},{24,16},{16,8},{8,0},{9,17},{... | collective-permute-start | bytes 1179656 | tf_op jit(solution)/shard_map/ppermute | solution.py:304
  177.4 8.5 %collective-permute-start.77 = (f32[200,512]{1,0:T(8,128)S(1)}, f32[200,512]{1,0:T(8,128)S(1)}, u32[]{:S(2)}, u32[]{:S(2)}) collective-permute-start(f32[200,512]{1,0:T(8,128)S(1)} %add.177), channel_id=1, source_target_pairs={{0,4},{4,12},{12,20},{20,28},{28,24},{24,16},{16,8},{8,0},{9,17},{... | collective-permute-start | bytes 1228808 | tf_op jit(solution)/shard_map/ppermute | solution.py:304
  181.6 8.6 %collective-permute-start.72 = (f32[3,64,512]{2,1,0:T(8,128)S(1)}, f32[3,64,512]{2,1,0:T(8,128)S(1)}, u32[]{:S(2)}, u32[]{:S(2)}) collective-permute-start(f32[3,64,512]{2,1,0:T(8,128)S(1)} %collective-permute-done.71.turn_ref), channel_id=1, source_target_pairs={{0,4},{4,12},{12,20},{20,28},{28,24},{24,16},{16,8},{8,0},{9,17},{... | collective-permute-start | bytes 1179656 | tf_op jit(solution)/shard_map/ppermute | solution.py:304
  186.0 8.5 %collective-permute-start.78 = (f32[200,512]{1,0:T(8,128)S(1)}, f32[200,512]{1,0:T(8,128)S(1)}, u32[]{:S(2)}, u32[]{:S(2)}) collective-permute-start(f32[200,512]{1,0:T(8,128)S(1)} %add.178), channel_id=1, source_target_pairs={{0,4},{4,12},{12,20},{20,28},{28,24},{24,16},{16,8},{8,0},{9,17},{... | collective-permute-start | bytes 1228808 | tf_op jit(solution)/shard_map/ppermute | solution.py:304
  194.6 8.0 %collective-permute-start.79 = (f32[200,512]{1,0:T(8,128)S(1)}, f32[200,512]{1,0:T(8,128)S(1)}, u32[]{:S(2)}, u32[]{:S(2)}) collective-permute-start(f32[200,512]{1,0:T(8,128)S(1)} %add.179), channel_id=1, source_target_pairs={{0,4},{4,12},{12,20},{20,28},{28,24},{24,16},{16,8},{8,0},{9,17},{... | collective-permute-start | bytes 1228808 | tf_op jit(solution)/shard_map/ppermute | solution.py:304
  (52 other events, 606.8 us)

commit v3 on v2

--- a/solution.py
+++ b/solution.py
@@ -9,7 +9,8 @@
 
 EPSILON = 1e-06
 VMEM_BYTES = 16 * 1024 * 1024
-FIRST_VMEM, REST_VMEM = 60 * 1024 * 1024, 52 * 1024 * 1024
+TURN_SETS, BACK_SETS = 3, 2
+FIRST_VMEM, REST_VMEM = 60 * 1024 * 1024, 16 * 1024 * 1024
 f32, bf16 = jnp.float32, jnp.bfloat16
 
 
@@ -39,6 +40,12 @@
     at = sum(jnp.where(device == name, place, 0) for place, name in enumerate(order))
     place = lax.rem(at - sign * (1 + step) + 2 * count, count)
     return sum(jnp.where(place == i, name, 0) for i, name in enumerate(order))
+
+
+def cuts(rows, sets):
+    tiles = rows // 8
+    ends = [8 * (tiles * (i + 1) // sets) for i in range(sets)]
+    return list(zip([0] + ends[:-1], ends))
 
 
 def pair(x):
@@ -159,17 +166,14 @@
     new_ref[...] = update * (target / actual)
 
 
-def renorm_back_kernel(anchor_ref, gain_one_ref, gain_two_ref, *refs):
-    arrived, mine, updates, (turned_ref, direct_ref, gain_ref) = refs[:3], refs[3:6], refs[6:9], refs[9:]
-    for i in range(3):
-        anchor, update, cot = anchor_ref[i], updates[i][...], arrived[i][...] + mine[i][...]
-        target, actual = scales(update, anchor)
-        inner = jnp.sum(update * cot, axis=-1, keepdims=True)
-        ratio = target / actual
-        update_cot = ratio * cot - update * (inner * ratio / (actual * actual))
-        turned_ref[i] = -update_cot
-        direct_ref[i] = update_cot + anchor * (inner / (actual * target))
-    gain_ref[...] = gain_one_ref[...] + gain_two_ref[...]
+def renorm_back_kernel(which, arrived_ref, mine_ref, update_ref, anchor_ref, turned_ref, direct_ref):
+    anchor, update, cot = anchor_ref[which], update_ref[...], arrived_ref[...] + mine_ref[...]
+    target, actual = scales(update, anchor)
+    inner = jnp.sum(update * cot, axis=-1, keepdims=True)
+    ratio = target / actual
+    update_cot = ratio * cot - update * (inner * ratio / (actual * actual))
+    turned_ref[...] = -update_cot
+    direct_ref[...] = update_cot + anchor * (inner / (actual * target))
 
 
 def forward_pass(queries, gate_mat, up_mat, down_mat):
@@ -247,24 +251,28 @@
     return act * up, hidden_turn, cot_gate, cot_up, back * slope * up, back * act
 
 
-def update_back_kernel(factor, order, step, first, last, key_ref, value_ref, rate_ref, weights_ref, turn_ref, gathered_ref, gain_ref, *refs):
+def update_back_kernel(factor, order, step, first, last, key_ref, value_ref, rate_ref, weights_ref, gathered_ref, gain_one_ref, gain_two_ref, *refs):
+    turns_ref, refs = refs[:3], refs[3:]
     if first:
-        direct_ref, refs = refs[0], refs[1:]
+        direct_ref, refs = refs[:3], refs[3:]
     else:
         before_key_ref, before_value_ref, refs = refs[0], refs[1], refs[2:]
-    out_ref, grad_key_ref, grad_value_ref = refs[:3]
+    outs_ref, (grad_key_ref, grad_value_ref), refs = refs[:BACK_SETS], refs[BACK_SETS : BACK_SETS + 2], refs[BACK_SETS + 2 :]
     keys, values = key_ref[...], value_ref[...]
     rate = minus_rate(rate_ref, factor)
-    rows = weights_ref.shape[1]
-    weights, turns = [weights_ref[i] for i in range(3)], [turn_ref[i] for i in range(3)]
+    weights, turns = [weights_ref[i] for i in range(3)], [t[...] for t in turns_ref]
     hidden, hidden_turn, cot_gate, cot_up, cot_gate_turn, cot_up_turn = second_order(keys, values, rate, weights, turns)
     sums = sums_by([cot_gate, cot_up], keys) + sums_by([hidden_turn * rate], values)
-    for i, total in enumerate(sums):
-        total = total + gathered_ref[i]
-        out_ref[i * rows : (i + 1) * rows] = total + direct_ref[i] if first else total
-    gain = jnp.broadcast_to(gain_ref[...], (8, gain_ref.shape[1]))
-    piece = gain_ref.shape[1] // len(order)
-    out_ref[3 * rows :] = pltpu.roll(gain, lax.rem((len(order) - owner_at(order, step)) * piece, gain_ref.shape[1]), 1)
+    sums = [total + gathered_ref[i] for i, total in enumerate(sums)]
+    if first:
+        sums = [total + direct_ref[i][...] for i, total in enumerate(sums)]
+    gain = jnp.broadcast_to(gain_one_ref[...] + gain_two_ref[...], (8, gain_one_ref.shape[1]))
+    piece = gain.shape[1] // len(order)
+    sums.append(pltpu.roll(gain, lax.rem((len(order) - owner_at(order, step)) * piece, gain.shape[1]), 1))
+    packed, at = jnp.concatenate(sums, axis=0), 0
+    for out_ref in outs_ref:
+        out_ref[...] = packed[at : at + out_ref.shape[0]]
+        at += out_ref.shape[0]
     grad_key = three(nn, pair(jnp.concatenate([cot_gate, cot_up, cot_gate_turn, cot_up_turn], axis=1)), pair(jnp.concatenate([weights[0], weights[1], turns[0], turns[1]], axis=0)))
     grad_value = rate * three(nn, pair(jnp.concatenate([hidden_turn, hidden], axis=1)), pair(jnp.concatenate([weights[2], turns[2]], axis=0)))
     if not first:
@@ -272,15 +280,16 @@
     grad_key_ref[...] = grad_key.astype(grad_key_ref.dtype)
     grad_value_ref[...] = grad_value.astype(grad_value_ref.dtype)
     if last:
-        refs[3][...] = to_rows([jnp.sum(grad_value * values.astype(f32), axis=1, keepdims=True)])[:1]
-
-
-def finish_kernel(arrived_ref, mine_ref, weights_ref, gain_ref):
+        refs[0][...] = to_rows([jnp.sum(grad_value * values.astype(f32), axis=1, keepdims=True)])[:1]
+
+
+def finish_kernel(*refs):
+    arrived, mine, (weights_ref, gain_ref) = refs[:BACK_SETS], refs[BACK_SETS : 2 * BACK_SETS], refs[2 * BACK_SETS :]
     rows = weights_ref.shape[1]
+    total = jnp.concatenate([a[...] + m[...] for a, m in zip(arrived, mine)], axis=0)
     for i in range(3):
-        at = slice(i * rows, (i + 1) * rows)
-        weights_ref[i] = arrived_ref[at] + mine_ref[at]
-    gain_ref[...] = (arrived_ref[3 * rows :] + mine_ref[3 * rows :])[:1, : gain_ref.shape[1]]
+        weights_ref[i] = total[i * rows : (i + 1) * rows]
+    gain_ref[...] = total[3 * rows : 3 * rows + 1, : gain_ref.shape[1]]
 
 
 def call(kernel, outs, *args, in_hbm=0, scratch=(), name=None, micros=4, vmem=VMEM_BYTES):
@@ -314,7 +323,7 @@
     norm_width = heads * width
     token_f32, token_bf16, whole = ((tokens, width), f32), ((tokens, width), bf16), ((3, hidden, width), f32)
     hidden_f32, stats_shape, gain_shape = ((tokens, hidden), f32), ((8, tokens), f32), ((1, width), f32)
-    chunk, part, packed = ((3, rows, width), f32), ((rows, width), f32), ((3 * rows + 8, width), f32)
+    chunk, part = ((3, rows, width), f32), ((rows, width), f32)
 
     def scatter(parts):
         totals = list(parts[:3])
@@ -373,25 +382,31 @@
     )
     (grad_query_one,) = call(query_grad_kernel, [token_bf16], grad_gate, grad_up, old_weights, name="query_one")
 
-    turn, direct, gain = call(
-        renorm_back_kernel, [chunk, chunk, gain_shape], placed[-1], gain_one, gain_two, *arrived, *parts[-3:], *updates, name="renorm_back"
-    )
+    turned = [
+        call(partial(renorm_back_kernel, i), [part] * 2, arrived[i], parts[i - 3], updates[i], placed[-1], name="renorm_back") for i in range(3)
+    ]
+    turn, direct = [t[0] for t in turned], [t[1] for t in turned]
+    packed = [((end - start, width), f32) for start, end in cuts(3 * rows + 8, BACK_SETS)]
 
     def back_at(step, turned, before, first=False, last=False):
-        outs = [packed] + ([token_bf16, token_bf16, ((1, tokens), f32)] if last else [token_f32, token_f32])
-        return call(
-            partial(update_back_kernel, factor, order, step, first, last), outs, keys, values, log_rate, placed[step], turned, direct_parts[step], gain,
-            *before, name="update_back",
+        outs = packed + ([token_bf16, token_bf16, ((1, tokens), f32)] if last else [token_f32, token_f32])
+        outs = call(
+            partial(update_back_kernel, factor, order, step, first, last), outs, keys, values, log_rate, placed[step], direct_parts[step], gain_one, gain_two,
+            *turned, *before, name="update_back",
         )
-
-    own, *sums = back_at(chunks - 1, turn, [direct], first=True)
-    total, held = None, turn
+        return outs[:BACK_SETS], outs[BACK_SETS:]
+
+    own, sums = back_at(chunks - 1, turn, direct, first=True)
+    totals, held = None, turn if TURN_SETS == 3 else jnp.concatenate([t[None] for t in turn])
     for step in range(chunks - 1):
-        held = send(held)
-        mine_now, *sums = back_at(step, held, sums, last=step == chunks - 2)
-        total = send(mine_now if total is None else total + mine_now)
+        if TURN_SETS == 3:
+            held = [send(h) for h in held]
+        else:
+            held = send(held)
+        mine_now, sums = back_at(step, held if TURN_SETS == 3 else [held[i] for i in range(3)], sums, last=step == chunks - 2)
+        totals = [send(m if totals is None else totals[i] + m) for i, m in enumerate(mine_now)]
     grad_key, grad_value, grad_rate = sums
-    grad_weights, grad_gain = call(finish_kernel, [chunk, ((1, width // chunks), f32)], total, own, name="finish")
+    grad_weights, grad_gain = call(finish_kernel, [chunk, ((1, width // chunks), f32)], *totals, *own, name="finish")
     grad_query = jnp.stack([grad_query_one, grad_query_two])[:, :, None, :]
     return grad_query, grad_key[:, None, :], grad_value[:, None, :], grad_rate, grad_weights[None], grad_gain
 

time: 204 us -> 198 us (0.971)
  waiting for transfers between devices: 64.5 us -> 50.8 us
  starting transfers between devices: 102 us -> 112 us
    ppermute x77 -> x98, waiting for transfers between devices: 61.6 us -> 47.9 us  [send(): return lax.ppermute(x, ('ctx', 'head'), pairs)]
    ppermute x77 -> x98, starting transfers between devices: 100 us -> 110 us  [send(): return lax.ppermute(x, ('ctx', 'head'), pairs)]
    pallas_call x21 -> x23, Pallas kernels: 33.5 us -> 31.6 us  [call(): pl.pallas_call(kernel, out_shape=[jax.ShapeDtypeStruct(shape, dtype) for...]
  transfers between devices with their start and end apart: 80 -> 101, of which waited for: 62 -> 67; matrix products, arithmetic and copies ran while one was open for 1% -> 1% of each run, Pallas kernels for 12% -> 12%
where the time goes in v3:
time: 198 us
  starting transfers between devices  112 us (57%)
  waiting for transfers between devices  50.8 us (26%)
  Pallas kernels  31.6 us (16%)
    ppermute x98, starting transfers between devices, send(): return lax.ppermute(x, ('ctx', 'head'), pairs)  110 us
    ppermute x98, waiting for transfers between devices, send(): return lax.ppermute(x, ('ctx', 'head'), pairs)  47.9 us
    pallas_call x23, Pallas kernels, call(): pl.pallas_call(kernel, out_shape=[jax.ShapeDtypeStruct(shape, dtype) for...  31.6 us
  transfers between devices with their start and end apart: 101, of which 67 were waited for; matrix products, arithmetic and copies ran while one was open for 1% of the time, Pallas kernels for 12%

profile of v3, /device:TPU:0, one launch (start us, length us, event | category | flops | bytes accessed | tf_op | source)
XLA Modules:
  0.0 197.8 jit_solution(6960480959475243496)
XLA Ops:
  0.7 3.8 %update.2 = (f32[64,512]{1,0:T(8,128)}, f32[64,512]{1,0:T(8,128)}, f32[64,512]{1,0:T(8,128)}, f32[3,64,512]{2,1,0:T(8,128)}) custom-call(f32[3,512,512]{2,1,0:T(8,128)} %bitcast.22, bf16[256,512]{1,0:T(8,128)(2,1)} %bitcast.24, bf16[256,512]{1,0:T(8,128)(2,1)} %bitcast.34, f32[1,256]{1,0:T(1,128)} %rate_ref.19), custom_call_target="tpu_custom_call" | custom-call | flops 4000000000 | bytes 12000000 | tf_op jit(solution)/shard_map/update/pallas_call | solution.py:297
  4.5 3.0 %collective-permute-start = (f32[64,512]{1,0:T(8,128)}, f32[64,512]{1,0:T(8,128)S(1)}, u32[]{:S(2)}, u32[]{:S(2)}) collective-permute-start(f32[64,512]{1,0:T(8,128)} %get-tuple-element.142), channel_id=1, source_target_pairs={{0,4},{4,12},{12,20},{20,28},{28,24},{24,16},{16,8},{8,0},{9,17},{... | collective-permute-start | bytes 393224 | tf_op jit(solution)/shard_map/ppermute | solution.py:313
  7.5 1.6 collective-permute-start.8
  9.1 1.6 collective-permute-start.16
  10.6 3.3 %update.3 = (f32[64,512]{1,0:T(8,128)S(1)}, f32[64,512]{1,0:T(8,128)S(1)}, f32[64,512]{1,0:T(8,128)S(1)}, f32[64,512]{1,0:T(8,128)S(1)}, f32[64,512]{1,0:T(8,128...) custom-call(f32[3,512,512]{2,1,0:T(8,128)S(1)} %bitcast.23, ...), custom_call_target="tpu_custom_call" | custom-call | flops 4000000000 | bytes 12000000 | tf_op jit(solution)/shard_map/update/pallas_call | solution.py:297
  14.0 1.6 collective-permute-start.1
  16.8 2.2 %collective-permute-done.1 = f32[64,512]{1,0:T(8,128)S(1)} collective-permute-done((f32[64,512]{1,0:T(8,128)S(1)}, f32[64,512]{1,0:T(8,128)S(1)}, u32[]{:S(2)}, u32[]{:S(2)}) %collective-permute-start.1) | collective-permute-done | bytes 131104 | tf_op jit(solution)/shard_map/ppermute | solution.py:313
  19.1 1.6 collective-permute-start.2
  22.1 1.4 collective-permute-start.18
  24.1 1.6 collective-permute-start.3
  25.8 1.4 collective-permute-start.11
  27.2 1.4 collective-permute-start.19
  29.2 1.6 collective-permute-start.4
  32.2 1.4 collective-permute-start.20
  34.2 1.6 collective-permute-start.5
  37.3 1.4 collective-permute-start.21
  39.2 1.6 collective-permute-start.6
  42.3 1.4 collective-permute-start.22
  44.4 1.6 collective-permute-start.7
  49.4 1.6 collective-permute-start.24
  54.4 1.6 collective-permute-start.27
  59.4 1.6 collective-permute-start.30
  64.3 1.6 collective-permute-start.33
  69.3 1.6 collective-permute-start.36
  74.3 1.6 collective-permute-start.39
  78.7 1.6 forward_one.1
  81.0 1.4 collective-permute-done.41.refs_21_
  82.4 1.6 forward_two.1
  84.1 1.6 collective-permute-start.43
  85.9 2.0 collective-permute-done.43
  88.8 2.3 %backward_two.1 = (f32[256,512]{1,0:T(8,128)S(1)}, f32[256,512]{1,0:T(8,128)S(1)}, f32[1,512]{1,0:T(1,128)S(1)}, f32[64,512]{1,0:T(8,128)S(1)}, f32[64,512]{1,0:...) custom-call(bf16[256,512]{1,0:T(8,128)(2,1)S(1)} %get-tuple-element., ...), custom_call_target="tpu_custom_call" | custom-call | flops 4000000000 | bytes 12000000 | tf_op jit(solution)/shard_map/backward_two/pallas_call | solution.py:297
  93.3 2.8 %collective-permute-done.45 = f32[64,512]{1,0:T(8,128)S(1)} collective-permute-done((f32[64,512]{1,0:T(8,128)S(1)}, f32[64,512]{1,0:T(8,128)S(1)}, u32[]{:S(2)}, u32[]{:S(2)}) %collective-permute-start.45) | collective-permute-done | bytes 131104 | tf_op jit(solution)/shard_map/ppermute | solution.py:313
  117.5 2.2 %backward_one.1 = (f32[256,512]{1,0:T(8,128)S(1)}, f32[256,512]{1,0:T(8,128)S(1)}, f32[1,512]{1,0:T(1,128)S(1)}, f32[3,64,512]{2,1,0:T(8,128)S(1)}, f32[3,64,512...) custom-call(bf16[256,512]{1,0:T(8,128)(2,1)S(1)} %get-tuple-element., ...), custom_call_target="tpu_custom_call" | custom-call | flops 4000000000 | bytes 12000000 | tf_op jit(solution)/shard_map/backward_one/pallas_call | solution.py:297
  128.4 1.5 collective-permute-done.65.arrived_ref
  132.0 1.5 update_back.8
  137.0 1.5 update_back.9
  143.8 1.5 update_back.10
  151.3 1.5 update_back.11
  154.2 2.4 %collective-permute-done.55.refs_0_ = f32[64,512]{1,0:T(8,128)S(1)} collective-permute-done((f32[64,512]{1,0:T(8,128)S(1)}, f32[64,512]{1,0:T(8,128)S(1)}, u32[]{:S(2)}, u32[]{:S(2)}) %collective-permute-start.55) | collective-permute-done | bytes 131104 | tf_op jit(solution)/shard_map/ppermute | solution.py:313
  161.3 1.5 update_back.12
  168.9 1.5 update_back.13
  175.1 1.5 collective-permute-done.97
  177.2 1.5 update_back.14
  178.8 4.1 %collective-permute-done.91 = f32[96,512]{1,0:T(8,128)S(1)} collective-permute-done((f32[96,512]{1,0:T(8,128)S(1)}, f32[96,512]{1,0:T(8,128)S(1)}, u32[]{:S(2)}, u32[]{:S(2)}) %collective-permute-start.91) | collective-permute-done | bytes 196640 | tf_op jit(solution)/shard_map/ppermute | solution.py:313
  183.5 1.6 collective-permute-done.98
  185.8 2.3 %update_back.15 = (f32[96,512]{1,0:T(8,128)S(1)}, f32[104,512]{1,0:T(8,128)S(1)}, bf16[256,512]{1,0:T(8,128)(2,1)}, bf16[256,512]{1,0:T(8,128)(2,1)}, f32[1,256]{1,0:T(1,128)}) custom-call(bf16[256,512]{1,0:T(8,128)(2,1)S(1)} %bitcast.33, bf16[256,512]{1,0:T(8,128)(2,1)S(1)} %bitcast.43, f32[1,256]{1,0:T(1,128)S(1)} %copy-done.4, ...), custom_call_target="tpu_custom_call" | custom-call | flops 4000000000 | bytes 12000000 | tf_op jit(solution)/shard_map/update_back/pallas_call | solution.py:297
  189.4 1.6 collective-permute-done.99
  194.4 2.6 %collective-permute-done.100.refs_1_ = f32[104,512]{1,0:T(8,128)S(1)} collective-permute-done((f32[104,512]{1,0:T(8,128)S(1)}, f32[104,512]{1,0:T(8,128)S(1)}, u32[]{:S(2)}, u32[]{:S(2)}) %collective-permute-start.100) | collective-permute-done | bytes 213024 | tf_op jit(solution)/shard_map/ppermute | solution.py:313
  (244 shorter events, 108.2 us)
Async XLA Ops:
  4.5 9.5 %collective-permute-start = (f32[64,512]{1,0:T(8,128)}, f32[64,512]{1,0:T(8,128)S(1)}, u32[]{:S(2)}, u32[]{:S(2)}) collective-permute-start(f32[64,512]{1,0:T(8,128)} %get-tuple-element.142), channel_id=1, source_target_pairs={{0,4},{4,12},{12,20},{20,28},{28,24},{24,16},{16,8},{8,0},{9,17},{... | collective-permute-start | bytes 393224 | tf_op jit(solution)/shard_map/ppermute | solution.py:313
  7.5 8.2 %collective-permute-start.8 = (f32[64,512]{1,0:T(8,128)}, f32[64,512]{1,0:T(8,128)S(1)}, u32[]{:S(2)}, u32[]{:S(2)}) collective-permute-start(f32[64,512]{1,0:T(8,128)} %get-tuple-element.151), channel_id=1, source_target_pairs={{0,4},{4,12},{12,20},{20,28},{28,24},{24,16},{16,8},{8,0},{9,17},{... | collective-permute-start | bytes 393224 | tf_op jit(solution)/shard_map/ppermute | solution.py:313
  9.1 7.2 %collective-permute-start.16 = (f32[64,512]{1,0:T(8,128)}, f32[64,512]{1,0:T(8,128)S(1)}, u32[]{:S(2)}, u32[]{:S(2)}) collective-permute-start(f32[64,512]{1,0:T(8,128)} %get-tuple-element.160), channel_id=1, source_target_pairs={{0,4},{4,12},{12,20},{20,28},{28,24},{24,16},{16,8},{8,0},{9,17},{... | collective-permute-start | bytes 393224 | tf_op jit(solution)/shard_map/ppermute | solution.py:313
  16.3 5.8 %collective-permute-start.17 = (f32[64,512]{1,0:T(8,128)S(1)}, f32[64,512]{1,0:T(8,128)S(1)}, u32[]{:S(2)}, u32[]{:S(2)}) collective-permute-start(f32[64,512]{1,0:T(8,128)S(1)} %add.165), channel_id=1, source_target_pairs={{0,4},{4,12},{12,20},{20,28},{28,24},{24,16},{16,8},{8,0},{9,17},{... | collective-permute-start | bytes 393224 | tf_op jit(solution)/shard_map/ppermute | solution.py:313
  40.9 5.1 %collective-permute-start.14 = (f32[64,512]{1,0:T(8,128)S(1)}, f32[64,512]{1,0:T(8,128)S(1)}, u32[]{:S(2)}, u32[]{:S(2)}) collective-permute-start(f32[64,512]{1,0:T(8,128)S(1)} %add.164), channel_id=1, source_target_pairs={{0,4},{4,12},{12,20},{20,28},{28,24},{24,16},{16,8},{8,0},{9,17},{... | collective-permute-start | bytes 393224 | tf_op jit(solution)/shard_map/ppermute | solution.py:313
  42.3 5.1 %collective-permute-start.22 = (f32[64,512]{1,0:T(8,128)S(1)}, f32[64,512]{1,0:T(8,128)S(1)}, u32[]{:S(2)}, u32[]{:S(2)}) collective-permute-start(f32[64,512]{1,0:T(8,128)S(1)} %add.170), channel_id=1, source_target_pairs={{0,4},{4,12},{12,20},{20,28},{28,24},{24,16},{16,8},{8,0},{9,17},{... | collective-permute-start | bytes 393224 | tf_op jit(solution)/shard_map/ppermute | solution.py:313
  74.3 6.0 %collective-permute-start.39 = (f32[64,512]{1,0:T(8,128)S(1)}, f32[64,512]{1,0:T(8,128)S(1)}, u32[]{:S(2)}, u32[]{:S(2)}) collective-permute-start(f32[64,512]{1,0:T(8,128)S(1)} %collective-permute-done.36.refs_16_), channel_id=1, source_target_pairs={{0,4},{4,12},{12,20},{20,28},{28,24},{24,16},{16,8},{8,0},{9,17},{... | collective-permute-start | bytes 393224 | tf_op jit(solution)/shard_map/ppermute | solution.py:313
  92.3 5.2 %collective-permute-start.59 = (f32[64,512]{1,0:T(8,128)S(1)}, f32[64,512]{1,0:T(8,128)S(1)}, u32[]{:S(2)}, u32[]{:S(2)}) collective-permute-start(f32[64,512]{1,0:T(8,128)S(1)} %get-tuple-element.195), channel_id=1, source_target_pairs={{0,4},{4,12},{12,20},{20,28},{28,24},{24,16},{16,8},{8,0},{9,17},{... | collective-permute-start | bytes 393224 | tf_op jit(solution)/shard_map/ppermute | solution.py:313
  92.9 6.0 %collective-permute-start.73 = (f32[64,512]{1,0:T(8,128)S(1)}, f32[64,512]{1,0:T(8,128)S(1)}, u32[]{:S(2)}, u32[]{:S(2)}) collective-permute-start(f32[64,512]{1,0:T(8,128)S(1)} %get-tuple-element.205), channel_id=1, source_target_pairs={{0,4},{4,12},{12,20},{20,28},{28,24},{24,16},{16,8},{8,0},{9,17},{... | collective-permute-start | bytes 393224 | tf_op jit(solution)/shard_map/ppermute | solution.py:313
  98.9 5.0 %collective-permute-start.74 = (f32[64,512]{1,0:T(8,128)S(1)}, f32[64,512]{1,0:T(8,128)S(1)}, u32[]{:S(2)}, u32[]{:S(2)}) collective-permute-start(f32[64,512]{1,0:T(8,128)S(1)} %add.186), channel_id=1, source_target_pairs={{0,4},{4,12},{12,20},{20,28},{28,24},{24,16},{16,8},{8,0},{9,17},{... | collective-permute-start | bytes 393224 | tf_op jit(solution)/shard_map/ppermute | solution.py:313
  112.7 7.1 %collective-permute-start.63 = (f32[64,512]{1,0:T(8,128)S(1)}, f32[64,512]{1,0:T(8,128)S(1)}, u32[]{:S(2)}, u32[]{:S(2)}) collective-permute-start(f32[64,512]{1,0:T(8,128)S(1)} %add.183), channel_id=1, source_target_pairs={{0,4},{4,12},{12,20},{20,28},{28,24},{24,16},{16,8},{8,0},{9,17},{... | collective-permute-start | bytes 393224 | tf_op jit(solution)/shard_map/ppermute | solution.py:313
  114.1 6.4 %collective-permute-start.77 = (f32[64,512]{1,0:T(8,128)S(1)}, f32[64,512]{1,0:T(8,128)S(1)}, u32[]{:S(2)}, u32[]{:S(2)}) collective-permute-start(f32[64,512]{1,0:T(8,128)S(1)} %add.189), channel_id=1, source_target_pairs={{0,4},{4,12},{12,20},{20,28},{28,24},{24,16},{16,8},{8,0},{9,17},{... | collective-permute-start | bytes 393224 | tf_op jit(solution)/shard_map/ppermute | solution.py:313
  120.4 5.8 %collective-permute-start.78 = (f32[64,512]{1,0:T(8,128)S(1)}, f32[64,512]{1,0:T(8,128)S(1)}, u32[]{:S(2)}, u32[]{:S(2)}) collective-permute-start(f32[64,512]{1,0:T(8,128)S(1)} %add.190), channel_id=1, source_target_pairs={{0,4},{4,12},{12,20},{20,28},{28,24},{24,16},{16,8},{8,0},{9,17},{... | collective-permute-start | bytes 393224 | tf_op jit(solution)/shard_map/ppermute | solution.py:313
  121.3 6.3 %collective-permute-start.51 = (f32[64,512]{1,0:T(8,128)S(1)}, f32[64,512]{1,0:T(8,128)S(1)}, u32[]{:S(2)}, u32[]{:S(2)}) collective-permute-start(f32[64,512]{1,0:T(8,128)S(1)} %add.179), channel_id=1, source_target_pairs={{0,4},{4,12},{12,20},{20,28},{28,24},{24,16},{16,8},{8,0},{9,17},{... | collective-permute-start | bytes 393224 | tf_op jit(solution)/shard_map/ppermute | solution.py:313
  126.3 5.0 %collective-permute-start.79 = (f32[64,512]{1,0:T(8,128)S(1)}, f32[64,512]{1,0:T(8,128)S(1)}, u32[]{:S(2)}, u32[]{:S(2)}) collective-permute-start(f32[64,512]{1,0:T(8,128)S(1)} %add.191), channel_id=1, source_target_pairs={{0,4},{4,12},{12,20},{20,28},{28,24},{24,16},{16,8},{8,0},{9,17},{... | collective-permute-start | bytes 393224 | tf_op jit(solution)/shard_map/ppermute | solution.py:313
  127.8 5.7 %collective-permute-start.52 = (f32[64,512]{1,0:T(8,128)S(1)}, f32[64,512]{1,0:T(8,128)S(1)}, u32[]{:S(2)}, u32[]{:S(2)}) collective-permute-start(f32[64,512]{1,0:T(8,128)S(1)} %get-tuple-element.194.refs_0_), channel_id=1, source_target_pairs={{0,4},{4,12},{12,20},{20,28},{28,24},{24,16},{16,8},{8,0},{9,17},{... | collective-permute-start | bytes 393224 | tf_op jit(solution)/shard_map/ppermute | solution.py:313
  133.6 6.8 %collective-permute-start.53 = (f32[64,512]{1,0:T(8,128)S(1)}, f32[64,512]{1,0:T(8,128)S(1)}, u32[]{:S(2)}, u32[]{:S(2)}) collective-permute-start(f32[64,512]{1,0:T(8,128)S(1)} %collective-permute-done.52.refs_0_), channel_id=1, source_target_pairs={{0,4},{4,12},{12,20},{20,28},{28,24},{24,16},{16,8},{8,0},{9,17},{... | collective-permute-start | bytes 393224 | tf_op jit(solution)/shard_map/ppermute | solution.py:313
  135.1 6.5 %collective-permute-start.67 = (f32[64,512]{1,0:T(8,128)S(1)}, f32[64,512]{1,0:T(8,128)S(1)}, u32[]{:S(2)}, u32[]{:S(2)}) collective-permute-start(f32[64,512]{1,0:T(8,128)S(1)} %collective-permute-done.66.refs_1_), channel_id=1, source_target_pairs={{0,4},{4,12},{12,20},{20,28},{28,24},{24,16},{16,8},{8,0},{9,17},{... | collective-permute-start | bytes 393224 | tf_op jit(solution)/shard_map/ppermute | solution.py:313
  136.5 6.3 %collective-permute-start.81 = (f32[64,512]{1,0:T(8,128)S(1)}, f32[64,512]{1,0:T(8,128)S(1)}, u32[]{:S(2)}, u32[]{:S(2)}) collective-permute-start(f32[64,512]{1,0:T(8,128)S(1)} %collective-permute-done.80.refs_2_), channel_id=1, source_target_pairs={{0,4},{4,12},{12,20},{20,28},{28,24},{24,16},{16,8},{8,0},{9,17},{... | collective-permute-start | bytes 393224 | tf_op jit(solution)/shard_map/ppermute | solution.py:313
  138.5 6.8 %collective-permute-start.87 = (f32[96,512]{1,0:T(8,128)S(1)}, f32[96,512]{1,0:T(8,128)S(1)}, u32[]{:S(2)}, u32[]{:S(2)}) collective-permute-start(f32[96,512]{1,0:T(8,128)S(1)} %get-tuple-element.242), channel_id=1, source_target_pairs={{0,4},{4,12},{12,20},{20,28},{28,24},{24,16},{16,8},{8,0},{9,17},{... | collective-permute-start | bytes 589832 | tf_op jit(solution)/shard_map/ppermute | solution.py:313
  139.2 7.4 %collective-permute-start.94 = (f32[104,512]{1,0:T(8,128)S(1)}, f32[104,512]{1,0:T(8,128)S(1)}, u32[]{:S(2)}, u32[]{:S(2)}) collective-permute-start(f32[104,512]{1,0:T(8,128)S(1)} %get-tuple-element.249), channel_id=1, source_target_pairs={{0,4},{4,12},{12,20},{20,28},{28,24},{24,16},{16,8},{8,0},{9,17},{... | collective-permute-start | bytes 638984 | tf_op jit(solution)/shard_map/ppermute | solution.py:313
  140.4 7.5 %collective-permute-start.54 = (f32[64,512]{1,0:T(8,128)S(1)}, f32[64,512]{1,0:T(8,128)S(1)}, u32[]{:S(2)}, u32[]{:S(2)}) collective-permute-start(f32[64,512]{1,0:T(8,128)S(1)} %collective-permute-done.53.refs_0_), channel_id=1, source_target_pairs={{0,4},{4,12},{12,20},{20,28},{28,24},{24,16},{16,8},{8,0},{9,17},{... | collective-permute-start | bytes 393224 | tf_op jit(solution)/shard_map/ppermute | solution.py:313
  141.6 7.7 %collective-permute-start.68 = (f32[64,512]{1,0:T(8,128)S(1)}, f32[64,512]{1,0:T(8,128)S(1)}, u32[]{:S(2)}, u32[]{:S(2)}) collective-permute-start(f32[64,512]{1,0:T(8,128)S(1)} %collective-permute-done.67.refs_1_), channel_id=1, source_target_pairs={{0,4},{4,12},{12,20},{20,28},{28,24},{24,16},{16,8},{8,0},{9,17},{... | collective-permute-start | bytes 393224 | tf_op jit(solution)/shard_map/ppermute | solution.py:313
  142.8 8.0 %collective-permute-start.82 = (f32[64,512]{1,0:T(8,128)S(1)}, f32[64,512]{1,0:T(8,128)S(1)}, u32[]{:S(2)}, u32[]{:S(2)}) collective-permute-start(f32[64,512]{1,0:T(8,128)S(1)} %collective-permute-done.81.refs_2_), channel_id=1, source_target_pairs={{0,4},{4,12},{12,20},{20,28},{28,24},{24,16},{16,8},{8,0},{9,17},{... | collective-permute-start | bytes 393224 | tf_op jit(solution)/shard_map/ppermute | solution.py:313
  145.3 7.5 %collective-permute-start.88 = (f32[96,512]{1,0:T(8,128)S(1)}, f32[96,512]{1,0:T(8,128)S(1)}, u32[]{:S(2)}, u32[]{:S(2)}) collective-permute-start(f32[96,512]{1,0:T(8,128)S(1)} %add.192), channel_id=1, source_target_pairs={{0,4},{4,12},{12,20},{20,28},{28,24},{24,16},{16,8},{8,0},{9,17},{... | collective-permute-start | bytes 589832 | tf_op jit(solution)/shard_map/ppermute | solution.py:313
  146.6 13.3 %collective-permute-start.95 = (f32[104,512]{1,0:T(8,128)S(1)}, f32[104,512]{1,0:T(8,128)S(1)}, u32[]{:S(2)}, u32[]{:S(2)}) collective-permute-start(f32[104,512]{1,0:T(8,128)S(1)} %add.198), channel_id=1, source_target_pairs={{0,4},{4,12},{12,20},{20,28},{28,24},{24,16},{16,8},{8,0},{9,17},{... | collective-permute-start | bytes 638984 | tf_op jit(solution)/shard_map/ppermute | solution.py:313
  147.9 8.6 %collective-permute-start.55 = (f32[64,512]{1,0:T(8,128)S(1)}, f32[64,512]{1,0:T(8,128)S(1)}, u32[]{:S(2)}, u32[]{:S(2)}) collective-permute-start(f32[64,512]{1,0:T(8,128)S(1)} %collective-permute-done.54.refs_0_), channel_id=1, source_target_pairs={{0,4},{4,12},{12,20},{20,28},{28,24},{24,16},{16,8},{8,0},{9,17},{... | collective-permute-start | bytes 393224 | tf_op jit(solution)/shard_map/ppermute | solution.py:313
  149.3 8.6 %collective-permute-start.69 = (f32[64,512]{1,0:T(8,128)S(1)}, f32[64,512]{1,0:T(8,128)S(1)}, u32[]{:S(2)}, u32[]{:S(2)}) collective-permute-start(f32[64,512]{1,0:T(8,128)S(1)} %collective-permute-done.68.refs_1_), channel_id=1, source_target_pairs={{0,4},{4,12},{12,20},{20,28},{28,24},{24,16},{16,8},{8,0},{9,17},{... | collective-permute-start | bytes 393224 | tf_op jit(solution)/shard_map/ppermute | solution.py:313
  150.7 8.6 %collective-permute-start.83 = (f32[64,512]{1,0:T(8,128)S(1)}, f32[64,512]{1,0:T(8,128)S(1)}, u32[]{:S(2)}, u32[]{:S(2)}) collective-permute-start(f32[64,512]{1,0:T(8,128)S(1)} %collective-permute-done.82.refs_2_), channel_id=1, source_target_pairs={{0,4},{4,12},{12,20},{20,28},{28,24},{24,16},{16,8},{8,0},{9,17},{... | collective-permute-start | bytes 393224 | tf_op jit(solution)/shard_map/ppermute | solution.py:313
  152.9 13.4 %collective-permute-start.89 = (f32[96,512]{1,0:T(8,128)S(1)}, f32[96,512]{1,0:T(8,128)S(1)}, u32[]{:S(2)}, u32[]{:S(2)}) collective-permute-start(f32[96,512]{1,0:T(8,128)S(1)} %add.193), channel_id=1, source_target_pairs={{0,4},{4,12},{12,20},{20,28},{28,24},{24,16},{16,8},{8,0},{9,17},{... | collective-permute-start | bytes 589832 | tf_op jit(solution)/shard_map/ppermute | solution.py:313
  156.5 6.3 %collective-permute-start.56 = (f32[64,512]{1,0:T(8,128)S(1)}, f32[64,512]{1,0:T(8,128)S(1)}, u32[]{:S(2)}, u32[]{:S(2)}) collective-permute-start(f32[64,512]{1,0:T(8,128)S(1)} %collective-permute-done.55.refs_0_), channel_id=1, source_target_pairs={{0,4},{4,12},{12,20},{20,28},{28,24},{24,16},{16,8},{8,0},{9,17},{... | collective-permute-start | bytes 393224 | tf_op jit(solution)/shard_map/ppermute | solution.py:313
  157.9 6.3 %collective-permute-start.70 = (f32[64,512]{1,0:T(8,128)S(1)}, f32[64,512]{1,0:T(8,128)S(1)}, u32[]{:S(2)}, u32[]{:S(2)}) collective-permute-start(f32[64,512]{1,0:T(8,128)S(1)} %collective-permute-done.69.refs_1_), channel_id=1, source_target_pairs={{0,4},{4,12},{12,20},{20,28},{28,24},{24,16},{16,8},{8,0},{9,17},{... | collective-permute-start | bytes 393224 | tf_op jit(solution)/shard_map/ppermute | solution.py:313
  159.3 6.3 %collective-permute-start.84 = (f32[64,512]{1,0:T(8,128)S(1)}, f32[64,512]{1,0:T(8,128)S(1)}, u32[]{:S(2)}, u32[]{:S(2)}) collective-permute-start(f32[64,512]{1,0:T(8,128)S(1)} %collective-permute-done.83.refs_2_), channel_id=1, source_target_pairs={{0,4},{4,12},{12,20},{20,28},{28,24},{24,16},{16,8},{8,0},{9,17},{... | collective-permute-start | bytes 393224 | tf_op jit(solution)/shard_map/ppermute | solution.py:313
  160.0 8.0 %collective-permute-start.96 = (f32[104,512]{1,0:T(8,128)S(1)}, f32[104,512]{1,0:T(8,128)S(1)}, u32[]{:S(2)}, u32[]{:S(2)}) collective-permute-start(f32[104,512]{1,0:T(8,128)S(1)} %add.199), channel_id=1, source_target_pairs={{0,4},{4,12},{12,20},{20,28},{28,24},{24,16},{16,8},{8,0},{9,17},{... | collective-permute-start | bytes 638984 | tf_op jit(solution)/shard_map/ppermute | solution.py:313
  162.9 7.5 %collective-permute-start.57 = (f32[64,512]{1,0:T(8,128)S(1)}, f32[64,512]{1,0:T(8,128)S(1)}, u32[]{:S(2)}, u32[]{:S(2)}) collective-permute-start(f32[64,512]{1,0:T(8,128)S(1)} %collective-permute-done.56.refs_0_), channel_id=1, source_target_pairs={{0,4},{4,12},{12,20},{20,28},{28,24},{24,16},{16,8},{8,0},{9,17},{... | collective-permute-start | bytes 393224 | tf_op jit(solution)/shard_map/ppermute | solution.py:313
  164.3 7.4 %collective-permute-start.71 = (f32[64,512]{1,0:T(8,128)S(1)}, f32[64,512]{1,0:T(8,128)S(1)}, u32[]{:S(2)}, u32[]{:S(2)}) collective-permute-start(f32[64,512]{1,0:T(8,128)S(1)} %collective-permute-done.70.refs_1_), channel_id=1, source_target_pairs={{0,4},{4,12},{12,20},{20,28},{28,24},{24,16},{16,8},{8,0},{9,17},{... | collective-permute-start | bytes 393224 | tf_op jit(solution)/shard_map/ppermute | solution.py:313
  165.7 7.0 %collective-permute-start.85 = (f32[64,512]{1,0:T(8,128)S(1)}, f32[64,512]{1,0:T(8,128)S(1)}, u32[]{:S(2)}, u32[]{:S(2)}) collective-permute-start(f32[64,512]{1,0:T(8,128)S(1)} %collective-permute-done.84.refs_2_), channel_id=1, source_target_pairs={{0,4},{4,12},{12,20},{20,28},{28,24},{24,16},{16,8},{8,0},{9,17},{... | collective-permute-start | bytes 393224 | tf_op jit(solution)/shard_map/ppermute | solution.py:313
  166.3 8.0 %collective-permute-start.90 = (f32[96,512]{1,0:T(8,128)S(1)}, f32[96,512]{1,0:T(8,128)S(1)}, u32[]{:S(2)}, u32[]{:S(2)}) collective-permute-start(f32[96,512]{1,0:T(8,128)S(1)} %add.194), channel_id=1, source_target_pairs={{0,4},{4,12},{12,20},{20,28},{28,24},{24,16},{16,8},{8,0},{9,17},{... | collective-permute-start | bytes 589832 | tf_op jit(solution)/shard_map/ppermute | solution.py:313
  168.0 8.6 %collective-permute-start.97 = (f32[104,512]{1,0:T(8,128)S(1)}, f32[104,512]{1,0:T(8,128)S(1)}, u32[]{:S(2)}, u32[]{:S(2)}) collective-permute-start(f32[104,512]{1,0:T(8,128)S(1)} %add.200), channel_id=1, source_target_pairs={{0,4},{4,12},{12,20},{20,28},{28,24},{24,16},{16,8},{8,0},{9,17},{... | collective-permute-start | bytes 638984 | tf_op jit(solution)/shard_map/ppermute | solution.py:313
  170.4 15.5 %collective-permute-start.58 = (f32[64,512]{1,0:T(8,128)S(1)}, f32[64,512]{1,0:T(8,128)S(1)}, u32[]{:S(2)}, u32[]{:S(2)}) collective-permute-start(f32[64,512]{1,0:T(8,128)S(1)} %collective-permute-done.57.refs_0_), channel_id=1, source_target_pairs={{0,4},{4,12},{12,20},{20,28},{28,24},{24,16},{16,8},{8,0},{9,17},{... | collective-permute-start | bytes 393224 | tf_op jit(solution)/shard_map/ppermute | solution.py:313
  171.6 14.2 %collective-permute-start.72 = (f32[64,512]{1,0:T(8,128)S(1)}, f32[64,512]{1,0:T(8,128)S(1)}, u32[]{:S(2)}, u32[]{:S(2)}) collective-permute-start(f32[64,512]{1,0:T(8,128)S(1)} %collective-permute-done.71.refs_1_), channel_id=1, source_target_pairs={{0,4},{4,12},{12,20},{20,28},{28,24},{24,16},{16,8},{8,0},{9,17},{... | collective-permute-start | bytes 393224 | tf_op jit(solution)/shard_map/ppermute | solution.py:313
  172.6 13.2 %collective-permute-start.86 = (f32[64,512]{1,0:T(8,128)S(1)}, f32[64,512]{1,0:T(8,128)S(1)}, u32[]{:S(2)}, u32[]{:S(2)}) collective-permute-start(f32[64,512]{1,0:T(8,128)S(1)} %collective-permute-done.85.refs_2_), channel_id=1, source_target_pairs={{0,4},{4,12},{12,20},{20,28},{28,24},{24,16},{16,8},{8,0},{9,17},{... | collective-permute-start | bytes 393224 | tf_op jit(solution)/shard_map/ppermute | solution.py:313
  174.3 8.6 %collective-permute-start.91 = (f32[96,512]{1,0:T(8,128)S(1)}, f32[96,512]{1,0:T(8,128)S(1)}, u32[]{:S(2)}, u32[]{:S(2)}) collective-permute-start(f32[96,512]{1,0:T(8,128)S(1)} %add.195), channel_id=1, source_target_pairs={{0,4},{4,12},{12,20},{20,28},{28,24},{24,16},{16,8},{8,0},{9,17},{... | collective-permute-start | bytes 589832 | tf_op jit(solution)/shard_map/ppermute | solution.py:313
  176.6 8.6 %collective-permute-start.98 = (f32[104,512]{1,0:T(8,128)S(1)}, f32[104,512]{1,0:T(8,128)S(1)}, u32[]{:S(2)}, u32[]{:S(2)}) collective-permute-start(f32[104,512]{1,0:T(8,128)S(1)} %add.201), channel_id=1, source_target_pairs={{0,4},{4,12},{12,20},{20,28},{28,24},{24,16},{16,8},{8,0},{9,17},{... | collective-permute-start | bytes 638984 | tf_op jit(solution)/shard_map/ppermute | solution.py:313
  182.9 5.7 %collective-permute-start.92 = (f32[96,512]{1,0:T(8,128)S(1)}, f32[96,512]{1,0:T(8,128)S(1)}, u32[]{:S(2)}, u32[]{:S(2)}) collective-permute-start(f32[96,512]{1,0:T(8,128)S(1)} %add.196), channel_id=1, source_target_pairs={{0,4},{4,12},{12,20},{20,28},{28,24},{24,16},{16,8},{8,0},{9,17},{... | collective-permute-start | bytes 589832 | tf_op jit(solution)/shard_map/ppermute | solution.py:313
  185.2 5.9 %collective-permute-start.99 = (f32[104,512]{1,0:T(8,128)S(1)}, f32[104,512]{1,0:T(8,128)S(1)}, u32[]{:S(2)}, u32[]{:S(2)}) collective-permute-start(f32[104,512]{1,0:T(8,128)S(1)} %add.202), channel_id=1, source_target_pairs={{0,4},{4,12},{12,20},{20,28},{28,24},{24,16},{16,8},{8,0},{9,17},{... | collective-permute-start | bytes 638984 | tf_op jit(solution)/shard_map/ppermute | solution.py:313
  188.7 5.7 %collective-permute-start.93 = (f32[96,512]{1,0:T(8,128)S(1)}, f32[96,512]{1,0:T(8,128)S(1)}, u32[]{:S(2)}, u32[]{:S(2)}) collective-permute-start(f32[96,512]{1,0:T(8,128)S(1)} %add.197), channel_id=1, source_target_pairs={{0,4},{4,12},{12,20},{20,28},{28,24},{24,16},{16,8},{8,0},{9,17},{... | collective-permute-start | bytes 589832 | tf_op jit(solution)/shard_map/ppermute | solution.py:313
  191.1 5.9 %collective-permute-start.100 = (f32[104,512]{1,0:T(8,128)S(1)}, f32[104,512]{1,0:T(8,128)S(1)}, u32[]{:S(2)}, u32[]{:S(2)}) collective-permute-start(f32[104,512]{1,0:T(8,128)S(1)} %add.203), channel_id=1, source_target_pairs={{0,4},{4,12},{12,20},{20,28},{28,24},{24,16},{16,8},{8,0},{9,17},{... | collective-permute-start | bytes 638984 | tf_op jit(solution)/shard_map/ppermute | solution.py:313
  (61 other events, 413.6 us)
